TPU v7x, 32 devices: a whole 2x2x4 slice. The times are simulated.
32 devices in a mesh: seg: 16 (over z, y, x), rep: 2 (over core).
Axes of the slice: x: 2, y: 2, z: 4, core: 2. Of those that a mesh axis runs over, the one named last changes fastest.
Arguments:
- tokens: bfloat16 [2, 64, 128, 768], P(None, ('seg', 'rep')), may hold values from -6 to 6
- token_counts: int32 [2, 64], replicated, may hold values from 0 to 128, as said below
- segment_project: bfloat16 [768, 2304], P(('seg', 'rep')), may hold values from -0.21875 to 0.21875
- segment_output: bfloat16 [768, 768], P(('seg', 'rep')), may hold values from -0.875 to 0.875
- segment_up: bfloat16 [768, 3072], P(('seg', 'rep')), may hold values from -0.21875 to 0.21875
- segment_down: bfloat16 [3072, 768], P(('seg', 'rep')), may hold values from -0.109375 to 0.109375
- segment_scale: bfloat16 [768], P(('seg', 'rep')), may hold values from 0.25 to 1.75
- segment_offset: bfloat16 [768], P(('seg', 'rep')), may hold values from -3 to 3
- segment_gain: bfloat16 [768], P(('seg', 'rep')), may hold values from 0.25 to 1.75
- segment_shift: bfloat16 [768], P(('seg', 'rep')), may hold values from -3 to 3
- document_project: bfloat16 [768, 2304], P(('seg', 'rep')), may hold values from -0.21875 to 0.21875
- document_output: bfloat16 [768, 768], P(('seg', 'rep')), may hold values from -0.875 to 0.875
- document_up: bfloat16 [768, 3072], P(('seg', 'rep')), may hold values from -0.21875 to 0.21875
- document_down: bfloat16 [3072, 768], P(('seg', 'rep')), may hold values from -0.109375 to 0.109375
- document_scale: bfloat16 [768], P(('seg', 'rep')), may hold values from 0.25 to 1.75
- document_offset: bfloat16 [768], P(('seg', 'rep')), may hold values from -3 to 3
- document_gain: bfloat16 [768], P(('seg', 'rep')), may hold values from 0.25 to 1.75
- document_shift: bfloat16 [768], P(('seg', 'rep')), may hold values from -3 to 3
- position: bfloat16 [768, 32], P(('seg', 'rep')), may hold values from -3 to 3
- cotangent: bfloat16 [2, 64, 128, 768], P(None, ('seg', 'rep')), may hold values from -6 to 6
Outputs:
- output: bfloat16 [2, 64, 128, 768], P(None, ('seg', 'rep'))
- input_gradient: float32 [2, 64, 128, 768], P(None, ('seg', 'rep'))
- segment_project_gradient: float32 [768, 2304], P(('seg', 'rep'))
- segment_output_gradient: float32 [768, 768], P(('seg', 'rep'))
- segment_up_gradient: float32 [768, 3072], P(('seg', 'rep'))
- segment_down_gradient: float32 [3072, 768], P(('seg', 'rep'))
- segment_scale_gradient: float32 [768], P(('seg', 'rep'))
- segment_offset_gradient: float32 [768], P(('seg', 'rep'))
- segment_gain_gradient: float32 [768], P(('seg', 'rep'))
- segment_shift_gradient: float32 [768], P(('seg', 'rep'))
- document_project_gradient: float32 [768, 2304], P(('seg', 'rep'))
- document_output_gradient: float32 [768, 768], P(('seg', 'rep'))
- document_up_gradient: float32 [768, 3072], P(('seg', 'rep'))
- document_down_gradient: float32 [3072, 768], P(('seg', 'rep'))
- document_scale_gradient: float32 [768], P(('seg', 'rep'))
- document_offset_gradient: float32 [768], P(('seg', 'rep'))
- document_gain_gradient: float32 [768], P(('seg', 'rep'))
- document_shift_gradient: float32 [768], P(('seg', 'rep'))
- position_gradient: float32 [768, 32], P(('seg', 'rep'))
Inputs may be any that keep to these rules, and one draw needn't show every extreme that they name: `token_counts`: within each document of 32 segments the counts are 128 up to one segment, which holds between 1 and 128 tokens, and 0 after it; the first segment of every document is full.
All inputs are finite; a program needn't handle non-finite values.
Results may differ from a plain program's by a relative error of at most 0.025.
Values may be sent and summed in bfloat16 or wider, within the bound.
A program may use at most 256 MiB of HBM per device.

v0:
```python
import math

import jax
import jax.numpy as jnp
from jax import lax
from jax.sharding import PartitionSpec as P

HEADS = 12
DOC_SEGS = 32


epsilon = 1e-05
floor_score = -1e30
root_half = 1.0 / math.sqrt(2.0)
inverse_root_tau = 1.0 / math.sqrt(2.0 * math.pi)


def partner_2(value, axis, distance):
    mask = 2**distance
    pairs = [(source, source ^ mask) for source in range(lax.axis_size(axis))]
    return lax.ppermute(value, axis, pairs)


def product(left, right):
    return jnp.dot(left, right, preferred_element_type=jnp.float32)


def left_product(left, right):
    return lax.dot_general(
        left, right, (((0,), (0,)), ((), ())), preferred_element_type=jnp.float32
    )


def right_product(left, right):
    return lax.dot_general(
        left, right, (((1,), (1,)), ((), ())), preferred_element_type=jnp.float32
    )


def gelu_value(value):
    return 0.5 * value * (1.0 + lax.erf(value * root_half))


def gelu_slope(value):
    return (
        0.5 * (1.0 + lax.erf(value * root_half))
        + value * jnp.exp(-0.5 * value * value) * inverse_root_tau
    )


def norm_forward(value, gain, shift):
    centred = value - jnp.mean(value, axis=-1, keepdims=True)
    inverse = lax.rsqrt(jnp.mean(centred * centred, axis=-1, keepdims=True) + epsilon)
    normed = centred * inverse
    return (normed * gain + shift, normed, inverse)


def norm_backward(delta_out, normed, inverse, gain):
    scaled = delta_out * gain
    delta_in = inverse * (
        scaled
        - jnp.mean(scaled, axis=-1, keepdims=True)
        - normed * jnp.mean(scaled * normed, axis=-1, keepdims=True)
    )
    return (delta_in, jnp.sum(delta_out * normed, axis=0), jnp.sum(delta_out, axis=0))


def masked_scores(queries, keys, valid):
    scale = 1.0 / math.sqrt(queries.shape[-1])
    scores = (
        jnp.einsum("bqhe,bkhe->bhqk", queries, keys, preferred_element_type=jnp.float32) * scale
    )
    return jnp.where(valid[:, None], scores, floor_score)


def attend_forward(queries, keys, values, valid):
    scores = masked_scores(queries, keys, valid)
    highest = jnp.max(scores, axis=-1, keepdims=True)
    log_total = highest + jnp.log(jnp.sum(jnp.exp(scores - highest), axis=-1, keepdims=True))
    shares = jnp.exp(scores - log_total).astype(jnp.bfloat16)
    context = jnp.einsum("bhqk,bkhe->bqhe", shares, values, preferred_element_type=jnp.float32)
    return (context.astype(jnp.bfloat16), log_total)


def attend_backward(delta_context, queries, keys, values, valid, log_total):
    scale = 1.0 / math.sqrt(queries.shape[-1])
    shares = jnp.exp(masked_scores(queries, keys, valid) - log_total)
    delta_shares = jnp.einsum(
        "bqhe,bkhe->bhqk", delta_context, values, preferred_element_type=jnp.float32
    )
    delta_values = jnp.einsum(
        "bhqk,bqhe->bkhe",
        shares.astype(jnp.bfloat16),
        delta_context,
        preferred_element_type=jnp.float32,
    )
    inner = jnp.sum(delta_shares * shares, axis=-1, keepdims=True)
    delta_scores = (shares * (delta_shares - inner)).astype(jnp.bfloat16)
    delta_queries = (
        jnp.einsum("bhqk,bkhe->bqhe", delta_scores, keys, preferred_element_type=jnp.float32)
        * scale
    )
    delta_keys = (
        jnp.einsum("bhqk,bqhe->bkhe", delta_scores, queries, preferred_element_type=jnp.float32)
        * scale
    )
    return (delta_queries, delta_keys, delta_values)


def block_forward(inputs, layer, attend):
    (
        project_weight,
        output_weight,
        up_weight,
        down_weight,
        first_gain,
        first_shift,
        second_gain,
        second_shift,
    ) = layer
    inputs_low = inputs.astype(jnp.bfloat16)
    projected = product(inputs_low, project_weight).astype(jnp.bfloat16)
    context, attend_kept = attend(projected)
    mixed = product(context, output_weight)
    first, first_normed, first_inverse = norm_forward(
        inputs + mixed, first_gain.astype(jnp.float32), first_shift.astype(jnp.float32)
    )
    first_low = first.astype(jnp.bfloat16)
    hidden = product(first_low, up_weight)
    active = gelu_value(hidden).astype(jnp.bfloat16)
    second, second_normed, second_inverse = norm_forward(
        first + product(active, down_weight),
        second_gain.astype(jnp.float32),
        second_shift.astype(jnp.float32),
    )
    kept = (
        inputs_low,
        projected,
        context,
        attend_kept,
        first_normed,
        first_inverse,
        first_low,
        hidden,
        active,
        second_normed,
        second_inverse,
    )
    return (second, kept)


def block_backward(delta_out, kept, layer, attend_back):
    (
        project_weight,
        output_weight,
        up_weight,
        down_weight,
        first_gain,
        first_shift,
        second_gain,
        second_shift,
    ) = layer
    (
        inputs_low,
        projected,
        context,
        attend_kept,
        first_normed,
        first_inverse,
        first_low,
        hidden,
        active,
        second_normed,
        second_inverse,
    ) = kept
    delta_second, second_gain_delta, second_shift_delta = norm_backward(
        delta_out, second_normed, second_inverse, second_gain.astype(jnp.float32)
    )
    branch_low = delta_second.astype(jnp.bfloat16)
    delta_down = left_product(active, branch_low)
    delta_hidden = (right_product(branch_low, down_weight) * gelu_slope(hidden)).astype(
        jnp.bfloat16
    )
    delta_up = left_product(first_low, delta_hidden)
    delta_first = delta_second + right_product(delta_hidden, up_weight)
    delta_mixed, first_gain_delta, first_shift_delta = norm_backward(
        delta_first, first_normed, first_inverse, first_gain.astype(jnp.float32)
    )
    mixed_low = delta_mixed.astype(jnp.bfloat16)
    delta_output = left_product(context, mixed_low)
    delta_context = right_product(mixed_low, output_weight).astype(jnp.bfloat16)
    delta_projected = attend_back(delta_context, projected, attend_kept)
    delta_project = left_product(inputs_low, delta_projected)
    delta_inputs = delta_mixed + right_product(delta_projected, project_weight)
    return (
        delta_inputs,
        (
            delta_project,
            delta_output,
            delta_up,
            delta_down,
            first_gain_delta,
            first_shift_delta,
            second_gain_delta,
            second_shift_delta,
        ),
    )


def local(
    tokens,
    token_counts,
    segment_project,
    segment_output,
    segment_up,
    segment_down,
    segment_scale,
    segment_offset,
    segment_gain,
    segment_shift,
    document_project,
    document_output,
    document_up,
    document_down,
    document_scale,
    document_offset,
    document_gain,
    document_shift,
    position,
    cotangent,
):
    batches, segments, length, width = tokens.shape
    heads = HEADS
    head_width = width // heads
    rows_total = segments * length
    index = lax.axis_index(("seg", "rep"))
    first_segment = index * segments
    own_document = first_segment // DOC_SEGS
    positions = jnp.arange(length)
    slots = (first_segment + jnp.arange(segments)) % DOC_SEGS
    picker = (slots[:, None] == jnp.arange(DOC_SEGS)[None, :]).astype(jnp.float32)
    levels = (DOC_SEGS // segments).bit_length() - 1
    gathered_once = (
        lax.all_gather(segment_project, ("seg", "rep"), axis=0, tiled=True),
        lax.all_gather(segment_output, ("seg", "rep"), axis=0, tiled=True),
        lax.all_gather(segment_up, ("seg", "rep"), axis=0, tiled=True),
        lax.all_gather(segment_down, ("seg", "rep"), axis=0, tiled=True),
        lax.all_gather(segment_scale, ("seg", "rep"), axis=0, tiled=True),
        lax.all_gather(segment_offset, ("seg", "rep"), axis=0, tiled=True),
        lax.all_gather(segment_gain, ("seg", "rep"), axis=0, tiled=True),
        lax.all_gather(segment_shift, ("seg", "rep"), axis=0, tiled=True),
        lax.all_gather(document_project, ("seg", "rep"), axis=0, tiled=True),
        lax.all_gather(document_output, ("seg", "rep"), axis=0, tiled=True),
        lax.all_gather(document_up, ("seg", "rep"), axis=0, tiled=True),
        lax.all_gather(document_down, ("seg", "rep"), axis=0, tiled=True),
        lax.all_gather(document_scale, ("seg", "rep"), axis=0, tiled=True),
        lax.all_gather(document_offset, ("seg", "rep"), axis=0, tiled=True),
        lax.all_gather(document_gain, ("seg", "rep"), axis=0, tiled=True),
        lax.all_gather(document_shift, ("seg", "rep"), axis=0, tiled=True),
        lax.all_gather(position, ("seg", "rep"), axis=0, tiled=True),
    )
    outputs = []
    deltas = []
    totals = None
    for batch in range(batches):
        segment_layer = gathered_once[0:8]
        document_layer = gathered_once[8:16]
        table = jnp.transpose(gathered_once[16].astype(jnp.float32))
        counts_row = token_counts[batch]
        local_counts = lax.dynamic_slice_in_dim(counts_row, first_segment, segments)
        token_valid = (positions[None, :] < local_counts[:, None]) | (positions[None, :] == 0)
        segment_valid = token_valid[:, None, :]

        def segment_attend(projected):
            parts = projected.reshape(segments, length, 3, heads, head_width)
            context, log_total = attend_forward(
                parts[:, :, 0], parts[:, :, 1], parts[:, :, 2], segment_valid
            )
            return (context.reshape(rows_total, width), log_total)

        def segment_back(delta_context, projected, log_total):
            parts = projected.reshape(segments, length, 3, heads, head_width)
            delta_queries, delta_keys, delta_values = attend_backward(
                delta_context.reshape(segments, length, heads, head_width),
                parts[:, :, 0],
                parts[:, :, 1],
                parts[:, :, 2],
                segment_valid,
                log_total,
            )
            return (
                jnp.stack((delta_queries, delta_keys, delta_values), axis=2)
                .reshape(rows_total, 3 * width)
                .astype(jnp.bfloat16)
            )

        def document_attend(projected):
            queries = projected[:, :width].reshape(1, segments, heads, head_width)
            pairs = projected[:, width:]
            collected = pairs[None]
            for bit in range(levels):
                partner = partner_2(collected, ("seg", "rep"), bit)
                upper = jnp.right_shift(index, bit) % 2
                collected = jnp.where(
                    upper == 0,
                    jnp.concatenate((collected, partner), axis=0),
                    jnp.concatenate((partner, collected), axis=0),
                )
            collected = collected.reshape(DOC_SEGS, 2 * width)
            key_valid = lax.dynamic_slice_in_dim(counts_row, own_document * DOC_SEGS, DOC_SEGS) > 0
            keys = collected[:, :width].reshape(1, DOC_SEGS, heads, head_width)
            values = collected[:, width:].reshape(1, DOC_SEGS, heads, head_width)
            valid = key_valid[None, None, :]
            context, log_total = attend_forward(queries, keys, values, valid)
            return (context.reshape(segments, width), (collected, valid, log_total))

        def document_back(delta_context, projected, kept_rows):
            collected, valid, log_total = kept_rows
            queries = projected[:, :width].reshape(1, segments, heads, head_width)
            keys = collected[:, :width].reshape(1, DOC_SEGS, heads, head_width)
            values = collected[:, width:].reshape(1, DOC_SEGS, heads, head_width)
            delta_queries, delta_keys, delta_values = attend_backward(
                delta_context.reshape(1, segments, heads, head_width),
                queries,
                keys,
                values,
                valid,
                log_total,
            )
            delta_pairs = jnp.concatenate(
                (delta_keys.reshape(DOC_SEGS, width), delta_values.reshape(DOC_SEGS, width)), axis=1
            )
            folded = delta_pairs.reshape(DOC_SEGS // segments, segments, 2 * width)
            for bit in reversed(range(levels)):
                halves = folded.reshape(2, folded.shape[0] // 2, segments, 2 * width)
                upper = jnp.right_shift(index, bit) % 2
                keep = jnp.where(upper == 0, halves[0], halves[1])
                send = jnp.where(upper == 0, halves[1], halves[0])
                folded = keep + partner_2(send.astype(jnp.bfloat16), ("seg", "rep"), bit).astype(
                    send.dtype
                )
            own_pairs = folded.reshape(segments, 2 * width)
            return jnp.concatenate(
                (delta_queries.reshape(segments, width), own_pairs), axis=1
            ).astype(jnp.bfloat16)

        inputs = tokens[batch].astype(jnp.float32).reshape(rows_total, width)
        segment_rows, segment_kept = block_forward(inputs, segment_layer, segment_attend)
        segment_rows = segment_rows.reshape(segments, length, width)
        lookup = jnp.sum(picker[:, :, None] * table[None, :, :], axis=1)
        summary_rows = segment_rows[:, 0, :] + lookup
        summary_out, document_kept = block_forward(summary_rows, document_layer, document_attend)
        outputs.append(segment_rows.at[:, 0, :].set(summary_out).astype(jnp.bfloat16))
        incoming = cotangent[batch].astype(jnp.float32)
        delta_summary, document_deltas = block_backward(
            incoming[:, 0, :], document_kept, document_layer, document_back
        )
        delta_table = jnp.transpose(jnp.sum(picker[:, :, None] * delta_summary[:, None, :], axis=0))
        delta_rows = incoming.at[:, 0, :].set(delta_summary).reshape(rows_total, width)
        delta_inputs, segment_deltas = block_backward(
            delta_rows, segment_kept, segment_layer, segment_back
        )
        deltas.append(delta_inputs.reshape(segments, length, width))
        current = segment_deltas + document_deltas + (delta_table,)
        totals = (
            current
            if totals is None
            else tuple((left + right for left, right in zip(totals, current)))
        )
    groups = lax.axis_size("seg")
    shaped = tuple(
        (item.reshape((groups, item.shape[0] // groups) + item.shape[1:]) for item in totals)
    )
    received = (
        lax.all_to_all(
            shaped[0].astype(jnp.bfloat16), "seg", split_axis=0, concat_axis=0, tiled=True
        ).astype(jnp.float32),
        lax.all_to_all(
            shaped[1].astype(jnp.bfloat16), "seg", split_axis=0, concat_axis=0, tiled=True
        ).astype(jnp.float32),
        lax.all_to_all(
            shaped[2].astype(jnp.bfloat16), "seg", split_axis=0, concat_axis=0, tiled=True
        ).astype(jnp.float32),
        lax.all_to_all(
            shaped[3].astype(jnp.bfloat16), "seg", split_axis=0, concat_axis=0, tiled=True
        ).astype(jnp.float32),
        lax.all_to_all(
            shaped[4].astype(jnp.bfloat16), "seg", split_axis=0, concat_axis=0, tiled=True
        ).astype(jnp.float32),
        lax.all_to_all(
            shaped[5].astype(jnp.bfloat16), "seg", split_axis=0, concat_axis=0, tiled=True
        ).astype(jnp.float32),
        lax.all_to_all(
            shaped[6].astype(jnp.bfloat16), "seg", split_axis=0, concat_axis=0, tiled=True
        ).astype(jnp.float32),
        lax.all_to_all(
            shaped[7].astype(jnp.bfloat16), "seg", split_axis=0, concat_axis=0, tiled=True
        ).astype(jnp.float32),
        lax.all_to_all(
            shaped[8].astype(jnp.bfloat16), "seg", split_axis=0, concat_axis=0, tiled=True
        ).astype(jnp.float32),
        lax.all_to_all(
            shaped[9].astype(jnp.bfloat16), "seg", split_axis=0, concat_axis=0, tiled=True
        ).astype(jnp.float32),
        lax.all_to_all(
            shaped[10].astype(jnp.bfloat16), "seg", split_axis=0, concat_axis=0, tiled=True
        ).astype(jnp.float32),
        lax.all_to_all(
            shaped[11].astype(jnp.bfloat16), "seg", split_axis=0, concat_axis=0, tiled=True
        ).astype(jnp.float32),
        lax.all_to_all(
            shaped[12].astype(jnp.bfloat16), "seg", split_axis=0, concat_axis=0, tiled=True
        ).astype(jnp.float32),
        lax.all_to_all(
            shaped[13].astype(jnp.bfloat16), "seg", split_axis=0, concat_axis=0, tiled=True
        ).astype(jnp.float32),
        lax.all_to_all(
            shaped[14].astype(jnp.bfloat16), "seg", split_axis=0, concat_axis=0, tiled=True
        ).astype(jnp.float32),
        lax.all_to_all(
            shaped[15].astype(jnp.bfloat16), "seg", split_axis=0, concat_axis=0, tiled=True
        ).astype(jnp.float32),
        lax.all_to_all(
            shaped[16].astype(jnp.bfloat16), "seg", split_axis=0, concat_axis=0, tiled=True
        ).astype(jnp.float32),
    )
    summed = tuple((jnp.sum(item, axis=0) for item in received))
    reduced = (
        lax.psum_scatter(
            summed[0].astype(jnp.bfloat16), "rep", scatter_dimension=0, tiled=True
        ).astype(jnp.float32),
        lax.psum_scatter(
            summed[1].astype(jnp.bfloat16), "rep", scatter_dimension=0, tiled=True
        ).astype(jnp.float32),
        lax.psum_scatter(
            summed[2].astype(jnp.bfloat16), "rep", scatter_dimension=0, tiled=True
        ).astype(jnp.float32),
        lax.psum_scatter(
            summed[3].astype(jnp.bfloat16), "rep", scatter_dimension=0, tiled=True
        ).astype(jnp.float32),
        lax.psum_scatter(
            summed[4].astype(jnp.bfloat16), "rep", scatter_dimension=0, tiled=True
        ).astype(jnp.float32),
        lax.psum_scatter(
            summed[5].astype(jnp.bfloat16), "rep", scatter_dimension=0, tiled=True
        ).astype(jnp.float32),
        lax.psum_scatter(
            summed[6].astype(jnp.bfloat16), "rep", scatter_dimension=0, tiled=True
        ).astype(jnp.float32),
        lax.psum_scatter(
            summed[7].astype(jnp.bfloat16), "rep", scatter_dimension=0, tiled=True
        ).astype(jnp.float32),
        lax.psum_scatter(
            summed[8].astype(jnp.bfloat16), "rep", scatter_dimension=0, tiled=True
        ).astype(jnp.float32),
        lax.psum_scatter(
            summed[9].astype(jnp.bfloat16), "rep", scatter_dimension=0, tiled=True
        ).astype(jnp.float32),
        lax.psum_scatter(
            summed[10].astype(jnp.bfloat16), "rep", scatter_dimension=0, tiled=True
        ).astype(jnp.float32),
        lax.psum_scatter(
            summed[11].astype(jnp.bfloat16), "rep", scatter_dimension=0, tiled=True
        ).astype(jnp.float32),
        lax.psum_scatter(
            summed[12].astype(jnp.bfloat16), "rep", scatter_dimension=0, tiled=True
        ).astype(jnp.float32),
        lax.psum_scatter(
            summed[13].astype(jnp.bfloat16), "rep", scatter_dimension=0, tiled=True
        ).astype(jnp.float32),
        lax.psum_scatter(
            summed[14].astype(jnp.bfloat16), "rep", scatter_dimension=0, tiled=True
        ).astype(jnp.float32),
        lax.psum_scatter(
            summed[15].astype(jnp.bfloat16), "rep", scatter_dimension=0, tiled=True
        ).astype(jnp.float32),
        lax.psum_scatter(
            summed[16].astype(jnp.bfloat16), "rep", scatter_dimension=0, tiled=True
        ).astype(jnp.float32),
    )
    return (jnp.stack(outputs), jnp.stack(deltas)) + tuple(reduced)


def solution(mesh):
    return jax.shard_map(
        local,
        mesh=mesh,
        in_specs=(
            P(None, ("seg", "rep"), None, None),
            P(),
            P(("seg", "rep"), None),
            P(("seg", "rep"), None),
            P(("seg", "rep"), None),
            P(("seg", "rep"), None),
            P(("seg", "rep")),
            P(("seg", "rep")),
            P(("seg", "rep")),
            P(("seg", "rep")),
            P(("seg", "rep"), None),
            P(("seg", "rep"), None),
            P(("seg", "rep"), None),
            P(("seg", "rep"), None),
            P(("seg", "rep")),
            P(("seg", "rep")),
            P(("seg", "rep")),
            P(("seg", "rep")),
            P(("seg", "rep"), None),
            P(None, ("seg", "rep"), None, None),
        ),
        out_specs=(
            P(None, ("seg", "rep"), None, None),
            P(None, ("seg", "rep"), None, None),
            P(("seg", "rep"), None),
            P(("seg", "rep"), None),
            P(("seg", "rep"), None),
            P(("seg", "rep"), None),
            P(("seg", "rep")),
            P(("seg", "rep")),
            P(("seg", "rep")),
            P(("seg", "rep")),
            P(("seg", "rep"), None),
            P(("seg", "rep"), None),
            P(("seg", "rep"), None),
            P(("seg", "rep"), None),
            P(("seg", "rep")),
            P(("seg", "rep")),
            P(("seg", "rep")),
            P(("seg", "rep")),
            P(("seg", "rep"), None),
        ),
        check_vma=False,
    )
```

profile of v0, /device:TPU:1, one launch (start us, length us, event | category | flops | bytes accessed | tf_op | source)
XLA Modules:
  0.0 1415.4 jit_solution(12379633464965690211)
XLA Ops:
  21.0 42.5 %all-reduce.17 = (bf16[768]{0:T(1024)(128)(2,1)S(1)}, bf16[768]{0:T(1024)(128)(2,1)S(1)}, bf16[768]{0:T(1024)(128)(2,1)S(1)}, bf16[768]{0:T(1024)(128)(2,1)S(1)}...) all-reduce(bf16[768]{0:T(1024)(128)(2,1)S(1)} %dynamic-update-slice, ...), channel_id=1, replica_groups=mesh['seg'=16,'rep'=2] {'seg','rep'}, use_global_device_ids=true, to_apply=%add.1 | all-reduce | flops 6144 | bytes 24576
  67.6 41.3 %all_gather.59 = bf16[768,32]{1,0:T(8,128)(2,1)S(1)} all-gather(bf16[24,32]{1,0:T(8,128)(2,1)} %param.46), channel_id=1, replica_groups=mesh['seg'=16,'rep'=2] {'seg','rep'}, dimensions={0}, use_global_device_ids=true | all-gather | bytes 50688 | tf_op jit(solution)/shard_map/all_gather | solution.py:260
  135.3 60.0 %all-gather.13.cloned.1.call-done = bf16[768,3072]{1,0:T(8,128)(2,1)} async-done(((bf16[24,3072]{1,0:T(8,128)(2,1)}), bf16[768,3072]{1,0:T(8,128)(2,1)}) %all-gather.13.cloned.1.call-update) | async-done | bytes 4718608 | tf_op jit(solution)/shard_map/all_gather | solution.py:246
  195.3 5.5 fusion.137
  200.8 59.8 %all-gather.15.cloned.1.call-done = bf16[3072,768]{1,0:T(8,128)(2,1)} async-done(((bf16[96,768]{1,0:T(8,128)(2,1)}), bf16[3072,768]{1,0:T(8,128)(2,1)}) %all-gather.15.cloned.1.call-update) | async-done | bytes 4718608 | tf_op jit(solution)/shard_map/all_gather | solution.py:247
  274.2 48.0 %all-gather.17.cloned.1.call-done = bf16[768,2304]{1,0:T(8,128)(2,1)} async-done(((bf16[24,2304]{1,0:T(8,128)(2,1)}), bf16[768,2304]{1,0:T(8,128)(2,1)}) %all-gather.17.cloned.1.call-update) | async-done | bytes 3538960 | tf_op jit(solution)/shard_map/all_gather | solution.py:252
  367.3 10.6 all-gather.19.cloned.1.call-done
  384.1 59.3 %all-gather.21.cloned.1.call-done = bf16[768,3072]{1,0:T(8,128)(2,1)} async-done(((bf16[24,3072]{1,0:T(8,128)(2,1)}), bf16[768,3072]{1,0:T(8,128)(2,1)}) %all-gather.21.cloned.1.call-update) | async-done | bytes 4718608 | tf_op jit(solution)/shard_map/all_gather | solution.py:254
  447.1 61.7 %all-gather.23.cloned.1.call-done = bf16[3072,768]{1,0:T(8,128)(2,1)} async-done(((bf16[96,768]{1,0:T(8,128)(2,1)}), bf16[3072,768]{1,0:T(8,128)(2,1)}) %all-gather.23.cloned.1.call-update) | async-done | bytes 4718608 | tf_op jit(solution)/shard_map/all_gather | solution.py:255
  565.0 5.8 fusion.121
  601.9 7.3 add_convert_fusion
  637.5 5.4 fusion
  651.6 5.3 all-to-all-start.12
  656.9 6.0 all-to-all-done.12
  667.1 5.4 all-to-all-done.13
  677.2 5.3 all-to-all-done.15
  686.7 5.3 all-to-all-done.7
  696.2 5.3 all-to-all-done.6
  738.6 12.3 all-to-all-done.9
  750.9 12.8 all-to-all-start.1
  768.0 15.3 %all-to-all-done.1 = bf16[16,48,768]{2,1,0:T(8,128)(2,1)S(1)} async-done(((bf16[16,48,768]{2,1,0:T(8,128)(2,1)}), bf16[16,48,768]{2,1,0:T(8,128)(2,1)S(1)}, u32[]{:S(2)}, u32[]{:S(2)}) %all-to-all-start.1) | async-done | bytes 1179680 | tf_op jit(solution)/shard_map/all_to_all | solution.py:378
  784.4 11.5 all-to-all-start.8
  822.5 40.2 %all-to-all-done.8 = bf16[16,48,2304]{2,1,0:T(8,128)(2,1)} async-done(((bf16[16,48,2304]{2,1,0:T(8,128)(2,1)}), bf16[16,48,2304]{2,1,0:T(8,128)(2,1)}, u32[]{:S(2)}, u32[]{:S(2)}) %all-to-all-start.8) | async-done | bytes 3538976 | tf_op jit(solution)/shard_map/all_to_all | solution.py:399
  862.7 94.5 %all_to_all.93 = bf16[16,48,2304]{2,1,0:T(8,128)(2,1)} all-to-all(bf16[16,48,2304]{2,1,0:T(8,128)(2,1)} %bitcast.367), channel_id=1, replica_groups=mesh['seg'=16,'rep'=2] {'seg'}, dimensions={0} | all-to-all | bytes 7077888 | tf_op jit(solution)/shard_map/all_to_all | solution.py:375
  967.5 82.1 %all-to-all-done.11 = bf16[16,192,768]{2,1,0:T(8,128)(2,1)} async-done(((bf16[16,192,768]{2,1,0:T(8,128)(2,1)}), bf16[16,192,768]{2,1,0:T(8,128)(2,1)}, u32[]{:S(2)}, u32[]{:S(2)}) %all-to-all-start.11) | async-done | bytes 4718624 | tf_op jit(solution)/shard_map/all_to_all | solution.py:408
  1049.6 21.5 %all-to-all-start.10 = ((bf16[16,48,3072]{2,1,0:T(8,128)(2,1)}), bf16[16,48,3072]{2,1,0:T(8,128)(2,1)}, u32[]{:S(2)}, u32[]{:S(2)}) async-start(bf16[16,48,3072]{2,1,0:T(8,128)(2,1)} %bitcast.364), calls=%async_computation.16 | async-start | bytes 9437184 | tf_op jit(solution)/shard_map/all_to_all | solution.py:405
  1076.6 81.4 %all-to-all-done.10 = bf16[16,48,3072]{2,1,0:T(8,128)(2,1)} async-done(((bf16[16,48,3072]{2,1,0:T(8,128)(2,1)}), bf16[16,48,3072]{2,1,0:T(8,128)(2,1)}, u32[]{:S(2)}, u32[]{:S(2)}) %all-to-all-start.10) | async-done | bytes 4718624 | tf_op jit(solution)/shard_map/all_to_all | solution.py:405
  1157.9 22.7 %all-to-all-start.2 = ((bf16[16,48,3072]{2,1,0:T(8,128)(2,1)}), bf16[16,48,3072]{2,1,0:T(8,128)(2,1)}, u32[]{:S(2)}, u32[]{:S(2)}) async-start(bf16[16,48,3072]{2,1,0:T(8,128)(2,1)} %bitcast.365), calls=%async_computation.4 | async-start | bytes 9437184 | tf_op jit(solution)/shard_map/all_to_all | solution.py:381
  1186.3 81.2 %all-to-all-done.2 = bf16[16,48,3072]{2,1,0:T(8,128)(2,1)} async-done(((bf16[16,48,3072]{2,1,0:T(8,128)(2,1)}), bf16[16,48,3072]{2,1,0:T(8,128)(2,1)}, u32[]{:S(2)}, u32[]{:S(2)}) %all-to-all-start.2) | async-done | bytes 4718624 | tf_op jit(solution)/shard_map/all_to_all | solution.py:381
  1267.5 22.7 %all-to-all-start.3 = ((bf16[16,192,768]{2,1,0:T(8,128)(2,1)}), bf16[16,192,768]{2,1,0:T(8,128)(2,1)}, u32[]{:S(2)}, u32[]{:S(2)}) async-start(bf16[16,192,768]{2,1,0:T(8,128)(2,1)} %bitcast.363), calls=%async_computation.6 | async-start | bytes 9437184 | tf_op jit(solution)/shard_map/all_to_all | solution.py:384
  1329.5 47.5 %all-to-all-done.3 = bf16[16,192,768]{2,1,0:T(8,128)(2,1)} async-done(((bf16[16,192,768]{2,1,0:T(8,128)(2,1)}), bf16[16,192,768]{2,1,0:T(8,128)(2,1)}, u32[]{:S(2)}, u32[]{:S(2)}) %all-to-all-start.3) | async-done | bytes 4718624 | tf_op jit(solution)/shard_map/all_to_all | solution.py:384
  1396.6 10.4 reduce-scatter.19.cloned.1.call-done
  (831 shorter events, 401.2 us)
Async XLA Ops:
  7.2 107.0 %all-gather.9.cloned.1.call-start = ((), (), s32[]{:S(2)}) async-start(), calls=%async_computation.26 | async-start | bytes 3649536 | tf_op jit(solution)/shard_map/all_gather | solution.py:244
  7.9 121.9 %all-gather.11.cloned.1.call-start = ((), (), s32[]{:S(2)}) async-start(), calls=%async_computation.27 | async-start | bytes 1216512 | tf_op jit(solution)/shard_map/all_gather | solution.py:245
  8.7 186.6 %all-gather.13.cloned.1.call-start = ((), (), s32[]{:S(2)}) async-start(), calls=%async_computation.28 | async-start | bytes 4866048 | tf_op jit(solution)/shard_map/all_gather | solution.py:246
  9.4 251.1 %all-gather.15.cloned.1.call-start = ((), (), s32[]{:S(2)}) async-start(), calls=%async_computation.29 | async-start | bytes 4866048 | tf_op jit(solution)/shard_map/all_gather | solution.py:247
  10.0 312.2 %all-gather.17.cloned.1.call-start = ((), (), s32[]{:S(2)}) async-start(), calls=%async_computation.30 | async-start | bytes 3649536 | tf_op jit(solution)/shard_map/all_gather | solution.py:252
  10.6 367.3 %all-gather.19.cloned.1.call-start = ((), (), s32[]{:S(2)}) async-start(), calls=%async_computation.31 | async-start | bytes 1216512 | tf_op jit(solution)/shard_map/all_gather | solution.py:253
  11.2 432.2 %all-gather.21.cloned.1.call-start = ((), (), s32[]{:S(2)}) async-start(), calls=%async_computation.32 | async-start | bytes 4866048 | tf_op jit(solution)/shard_map/all_gather | solution.py:254
  11.9 496.9 %all-gather.23.cloned.1.call-start = ((), (), s32[]{:S(2)}) async-start(), calls=%async_computation.33 | async-start | bytes 4866048 | tf_op jit(solution)/shard_map/all_gather | solution.py:255
  572.8 78.8 %all-to-all-start.14 = ((bf16[16,1,48]{2,1,0:T(2,128)(2,1)}), bf16[16,1,48]{2,1,0:T(2,128)(2,1)}, u32[]{:S(2)}, u32[]{:S(2)}) async-start(bf16[16,1,48]{2,1,0:T(2,128)(2,1)} %convert_element_type.712), calls=%async_computation.22 | async-start | bytes 16384 | tf_op jit(solution)/shard_map/all_to_all | solution.py:417
  592.4 20.6 %collective-permute-start.12 = (bf16[8,2,1536]{2,1,0:T(2,128)(2,1)}, bf16[8,2,1536]{2,1,0:T(2,128)(2,1)}, u32[]{:S(2)}, u32[]{:S(2)}) collective-permute-start(bf16[8,2,1536]{2,1,0:T(2,128)(2,1)} %convert_element_type.636), channel_id=1, source_target_pairs={{0,8},{1,9},{2,10},{3,11},{4,12},{5,13},{6,14},{7,15},{8,0},{9,1},... | collective-permute-start | bytes 147464 | tf_op jit(solution)/shard_map/ppermute | solution.py:21
  601.7 13.7 collective-permute-start.8
  651.6 11.3 all-to-all-start.12
  662.9 9.5 all-to-all-start.13
  682.5 9.5 all-to-all-start.7
  692.0 9.5 all-to-all-start.6
  720.5 9.8 all-to-all-start.16
  730.3 20.6 %all-to-all-start.9 = ((bf16[16,48,768]{2,1,0:T(8,128)(2,1)}), bf16[16,48,768]{2,1,0:T(8,128)(2,1)}, u32[]{:S(2)}, u32[]{:S(2)}) async-start(bf16[16,48,768]{2,1,0:T(8,128)(2,1)} %bitcast.372), calls=%async_computation.14 | async-start | bytes 2359296 | tf_op jit(solution)/shard_map/all_to_all | solution.py:402
  750.9 32.4 %all-to-all-start.1 = ((bf16[16,48,768]{2,1,0:T(8,128)(2,1)}), bf16[16,48,768]{2,1,0:T(8,128)(2,1)S(1)}, u32[]{:S(2)}, u32[]{:S(2)}) async-start(bf16[16,48,768]{2,1,0:T(8,128)(2,1)} %bitcast.373), calls=%async_computation.2 | async-start | bytes 2359296 | tf_op jit(solution)/shard_map/all_to_all | solution.py:378
  784.4 78.4 %all-to-all-start.8 = ((bf16[16,48,2304]{2,1,0:T(8,128)(2,1)}), bf16[16,48,2304]{2,1,0:T(8,128)(2,1)}, u32[]{:S(2)}, u32[]{:S(2)}) async-start(bf16[16,48,2304]{2,1,0:T(8,128)(2,1)} %bitcast.366), calls=%async_computation.12 | async-start | bytes 7077888 | tf_op jit(solution)/shard_map/all_to_all | solution.py:399
  957.2 92.4 %all-to-all-start.11 = ((bf16[16,192,768]{2,1,0:T(8,128)(2,1)}), bf16[16,192,768]{2,1,0:T(8,128)(2,1)}, u32[]{:S(2)}, u32[]{:S(2)}) async-start(bf16[16,192,768]{2,1,0:T(8,128)(2,1)} %bitcast.362), calls=%async_computation.18 | async-start | bytes 9437184 | tf_op jit(solution)/shard_map/all_to_all | solution.py:408
  1049.6 108.3 %all-to-all-start.10 = ((bf16[16,48,3072]{2,1,0:T(8,128)(2,1)}), bf16[16,48,3072]{2,1,0:T(8,128)(2,1)}, u32[]{:S(2)}, u32[]{:S(2)}) async-start(bf16[16,48,3072]{2,1,0:T(8,128)(2,1)} %bitcast.364), calls=%async_computation.16 | async-start | bytes 9437184 | tf_op jit(solution)/shard_map/all_to_all | solution.py:405
  1157.9 109.5 %all-to-all-start.2 = ((bf16[16,48,3072]{2,1,0:T(8,128)(2,1)}), bf16[16,48,3072]{2,1,0:T(8,128)(2,1)}, u32[]{:S(2)}, u32[]{:S(2)}) async-start(bf16[16,48,3072]{2,1,0:T(8,128)(2,1)} %bitcast.365), calls=%async_computation.4 | async-start | bytes 9437184 | tf_op jit(solution)/shard_map/all_to_all | solution.py:381
  1267.5 109.5 %all-to-all-start.3 = ((bf16[16,192,768]{2,1,0:T(8,128)(2,1)}), bf16[16,192,768]{2,1,0:T(8,128)(2,1)}, u32[]{:S(2)}, u32[]{:S(2)}) async-start(bf16[16,192,768]{2,1,0:T(8,128)(2,1)} %bitcast.363), calls=%async_computation.6 | async-start | bytes 9437184 | tf_op jit(solution)/shard_map/all_to_all | solution.py:384
  1290.2 94.1 %reduce-scatter.29.cloned.1.call-start = ((), (), s32[]{:S(2)}) async-start(), calls=%async_computation.42 | async-start | bytes 18432
  1291.2 94.5 %reduce-scatter.23.cloned.1.call-start = ((), (), s32[]{:S(2)}) async-start(), calls=%async_computation.39 | async-start | bytes 110592 | tf_op jit(solution)/shard_map/reduce_scatter | solution.py:456
  1293.5 93.6 %reduce-scatter.15.cloned.1.call-start = ((), (), s32[]{:S(2)}) async-start(), calls=%async_computation.35 | async-start | bytes 110592 | tf_op jit(solution)/shard_map/reduce_scatter | solution.py:432
  1295.6 92.8 %reduce-scatter.21.cloned.1.call-start = ((), (), s32[]{:S(2)}) async-start(), calls=%async_computation.38 | async-start | bytes 331776 | tf_op jit(solution)/shard_map/reduce_scatter | solution.py:453
  1299.0 91.1 %reduce-scatter.13.cloned.1.call-start = ((), (), s32[]{:S(2)}) async-start(), calls=%async_computation.34 | async-start | bytes 331776 | tf_op jit(solution)/shard_map/reduce_scatter | solution.py:429
  1300.4 91.3 %reduce-scatter.27.cloned.1.call-start = ((), (), s32[]{:S(2)}) async-start(), calls=%async_computation.41 | async-start | bytes 442368 | tf_op jit(solution)/shard_map/reduce_scatter | solution.py:462
  1304.3 88.9 %reduce-scatter.25.cloned.1.call-start = ((), (), s32[]{:S(2)}) async-start(), calls=%async_computation.40 | async-start | bytes 442368 | tf_op jit(solution)/shard_map/reduce_scatter | solution.py:459
  1310.5 84.5 %reduce-scatter.17.cloned.1.call-start = ((), (), s32[]{:S(2)}) async-start(), calls=%async_computation.36 | async-start | bytes 442368 | tf_op jit(solution)/shard_map/reduce_scatter | solution.py:435
  1319.7 87.3 %reduce-scatter.19.cloned.1.call-start = ((), (), s32[]{:S(2)}) async-start(), calls=%async_computation.37 | async-start | bytes 442368 | tf_op jit(solution)/shard_map/reduce_scatter | solution.py:438
  (226 other events, 3242.4 us)
Sparse Core Ops, SparseCore 0:
  10.9 63.2 all-gather.8
  77.1 52.6 all-gather.10
  132.7 62.5 all-gather.12
  198.0 62.4 all-gather.14
  263.3 58.8 all-gather.16
  324.9 52.9 all-gather.18
  380.8 62.5 all-gather.20
  446.3 62.4 all-gather.22
  1293.8 9.8 reduce-scatter.28
  1306.3 8.6 reduce-scatter.22
  1317.7 8.5 reduce-scatter.14
  1329.0 8.7 reduce-scatter.20
  1340.6 8.7 reduce-scatter.12
  1352.1 8.8 reduce-scatter.26
  1363.6 8.8 reduce-scatter.24
  1375.1 8.8 reduce-scatter.16
  1386.1 20.8 reduce-scatter.18
where the time goes:
time: 1430 us; the launch traced here: 1420 us
  waiting for transfers between devices  720 us (50%)
  blocking collectives  182 us (13%)
  matrix products  154 us (11%)
  starting transfers between devices  152 us (11%)
  local copies, waits for them, and re-layouts  105 us (7%)
  other arithmetic  83.3 us (6%)
  between operations  18.2 us (1%)
    all_to_all x1, blocking collectives, local(): lax.all_to_all(shaped[0].astype(jnp.bfloat16), 'seg', split_axis=0, conca...  94.5 us
    all_to_all x1, waiting for transfers between devices, local(): lax.all_to_all(shaped[11].astype(jnp.bfloat16), 'seg', split_axis=0, conc...  82.1 us
    all_to_all x1, waiting for transfers between devices, local(): lax.all_to_all(shaped[10].astype(jnp.bfloat16), 'seg', split_axis=0, conc...  81.4 us
    all_to_all x1, waiting for transfers between devices, local(): lax.all_to_all(shaped[2].astype(jnp.bfloat16), 'seg', split_axis=0, conca...  81.2 us
    all_gather x1, waiting for transfers between devices, local(): lax.all_gather(document_down, ('seg', 'rep'), axis=0, tiled=True)  61.7 us
    all_gather x1, waiting for transfers between devices, local(): lax.all_gather(segment_up, ('seg', 'rep'), axis=0, tiled=True)  60 us
    all_gather x1, waiting for transfers between devices, local(): lax.all_gather(segment_down, ('seg', 'rep'), axis=0, tiled=True)  59.8 us
    all_gather x1, waiting for transfers between devices, local(): lax.all_gather(document_up, ('seg', 'rep'), axis=0, tiled=True)  59.3 us
  transfers between devices with their start and end apart: 49, of which 30 were waited for; matrix products, arithmetic and copies ran while one was open for 19% of the time, Pallas kernels for 0%

commit v1 on v0

--- a/solution.py
+++ b/solution.py
@@ -1,18 +1,1046 @@
 import math
-
 import jax
 import jax.numpy as jnp
 from jax import lax
+from jax.experimental import pallas as pl
+from jax.experimental.pallas import tpu as pltpu
 from jax.sharding import PartitionSpec as P
 
+MESH = pl.DeviceIdType.MESH
+F32 = jnp.float32
+BF = jnp.bfloat16
 HEADS = 12
 DOC_SEGS = 32
-
-
 epsilon = 1e-05
 floor_score = -1e30
 root_half = 1.0 / math.sqrt(2.0)
 inverse_root_tau = 1.0 / math.sqrt(2.0 * math.pi)
+
+
+class Spot:
+    def __init__(self):
+        s, c = lax.axis_index("seg"), lax.axis_index("rep")
+        z, y, x = lax.div(s, 4), lax.rem(lax.div(s, 2), 2), lax.rem(s, 2)
+        self.s, self.c, self.z = s, c, z
+        self.o = 1 - c
+        y1, x1 = y + c * (1 - 2 * y), x + (1 - c) * (1 - 2 * x)
+        y2, x2 = y + (1 - c) * (1 - 2 * y), x + c * (1 - 2 * x)
+        self.q = 2 * y + x
+        self.q1 = 2 * y1 + x1
+        self.q2 = 2 * y2 + x2
+        self.q12 = 3 - self.q
+        self.sib = (s, 1 - c)
+        self.n1 = (4 * z + self.q1, c)
+        self.n2 = (4 * z + self.q2, c)
+        self.zz = [lax.rem(z + k, 4) for k in (1, 2, 3)]
+        self.zn = [(4 * zz + self.q, c) for zz in self.zz]
+        self.qq = [lax.rem(self.q + k, 4) for k in (0, 1, 2, 3)]
+        self.plane = [(4 * z + qq, c) for qq in self.qq]
+        self.half = lax.rem(z, 2)
+        self.zo = z + 1 - 2 * self.half
+        self.i = 8 * self.half + 2 * self.q + c
+        self.dev = 2 * s + c
+
+
+def remote(src, dst, ssem, rsem, dev):
+    return pltpu.make_async_remote_copy(
+        src_ref=src, dst_ref=dst, send_sem=ssem, recv_sem=rsem, device_id=dev, device_id_type=MESH
+    )
+
+
+def enter(t):
+    bar = pltpu.get_barrier_semaphore()
+    everyone = [t.sib]
+    for k in range(4):
+        for e in range(4):
+            if k or e:
+                s = 4 * lax.rem(t.z + k, 4) + lax.rem(t.q + e, 4)
+                everyone += [(s, t.c), (s, t.o)]
+    for dev in everyone:
+        pl.semaphore_signal(bar, inc=1, device_id=dev, device_id_type=MESH)
+    pl.semaphore_wait(bar, len(everyone))
+
+
+class Sender:
+    def __init__(self, t, ss, rs):
+        self.t, self.ss, self.rs, self.pending = t, ss, rs, []
+
+    def send(self, at, src, dst, dev):
+        d = remote(src, dst, self.ss.at[at], self.rs.at[at], dev)
+        d.start()
+        self.pending.append(d)
+
+    def arrived(self, at, ref):
+        remote(ref, ref, self.ss.at[at], self.rs.at[at], self.t.sib).wait_recv()
+
+    def drain(self):
+        for d in self.pending:
+            d.wait_send()
+        self.pending = []
+
+
+def off(at, size, step=128):
+    return pl.ds(pl.multiple_of(at * size, step), size)
+
+
+def join_pair(t, shard, got, tmp, dest):
+    rd, n2 = got.shape
+    wide = tmp.shape[1]
+    for j in range(0, n2, wide):
+        mine = pl.ds(pl.multiple_of(t.c * n2 + j, 128), wide)
+        tmp[off(t.c, rd, 8), :] = shard[:, mine].astype(F32)
+        tmp[off(t.o, rd, 8), :] = got[:, j : j + wide].astype(F32)
+        dest[:, pl.ds(j, wide)] = tmp[...].astype(dest.dtype)
+
+
+class Gather(Sender):
+    def __init__(self, t, shard, w, got, tmp, windows, ss, rs):
+        super().__init__(t, ss, rs)
+        self.shard, self.w, self.got, self.tmp, self.windows = shard, w, got, tmp, windows
+
+    def pair(self):
+        n2 = self.got.shape[1]
+        self.send((0, 0), self.shard.at[:, off(self.t.o, n2)], self.got, self.t.sib)
+
+    def join(self):
+        t = self.t
+        self.arrived((0, 0), self.got)
+        join_pair(t, self.shard, self.got, self.tmp, self.w.at[t.c, t.z, t.q])
+
+    def pick(self, k, *lead):
+        rows, cols = self.windows[k]
+        return self.w.at[(self.t.c,) + lead + (pl.ds(*rows), pl.ds(*cols))]
+
+    def line(self, k, q):
+        return self.pick(k, slice(None), q)
+
+    def spread(self, k):
+        t = self.t
+        own = self.pick(k, t.z, t.q)
+        for dev in t.zn:
+            self.send((k, 1), own, own, dev)
+
+    def first(self, k):
+        t = self.t
+        self.arrived((k, 1), self.pick(k, pl.ds(0, 3), t.q))
+        line = self.line(k, t.q)
+        self.send((k, 2), line, line, t.n1)
+        self.send((k, 4), line, line, t.sib)
+
+    def second(self, k):
+        t = self.t
+        line, other = self.line(k, t.q), self.line(k, t.q1)
+        self.arrived((k, 2), other)
+        self.send((k, 3), line, line, t.n2)
+        self.send((k, 7), other, other, t.n2)
+        self.send((k, 5), other, other, t.sib)
+
+    def third(self, k):
+        t = self.t
+        for i in (3, 7):
+            self.arrived((k, i), self.line(k, t.q))
+        for i, q in ((6, t.q2), (8, t.q12)):
+            self.send((k, i), self.line(k, q), self.line(k, q), t.sib)
+
+    def finish(self, k):
+        for i in (4, 5, 6, 8):
+            self.arrived((k, i), self.line(k, self.t.q))
+
+
+class DocGather(Sender):
+    def __init__(self, t, shards, stages, gots, tmps, dpu, do, dd, ss, rs, ls):
+        super().__init__(t, ss, rs)
+        self.shards, self.stages, self.gots, self.tmps = shards, stages, gots, tmps
+        self.dpu, self.do, self.dd, self.ls = dpu, do, dd, ls
+
+    def pair(self):
+        for i in range(2):
+            n2 = self.gots[i].shape[1]
+            self.send(i, self.shards[i].at[:, off(self.t.o, n2)], self.gots[i], self.t.sib)
+
+    def join(self):
+        t = self.t
+        for i in range(2):
+            self.arrived(i, self.gots[i])
+            join_pair(t, self.shards[i], self.gots[i], self.tmps[i], self.stages[i].at[t.z])
+
+    def spread(self, i):
+        own = self.stages[i].at[self.t.z]
+        for dev in self.t.zn:
+            self.send(2 + i, own, own, dev)
+
+    def plane(self):
+        t = self.t
+        main, down = self.stages
+        for i in range(2):
+            self.arrived(2 + i, self.stages[i].at[pl.ds(0, 3)])
+        self.local = []
+        for k in (1, 2, 3, 0):
+            q = t.qq[k]
+            moves = (
+                (main.at[:, :, off(q, 768)], self.dpu.at[t.c, :, t.q]),
+                (main.at[q, :, pl.ds(3072, 384)], self.do.at[t.c, pl.ds(pl.multiple_of(48 * t.q, 16), 48)]),
+                (down.at[q], self.dd.at[t.c, t.q]),
+            )
+            for i, (src, dst) in enumerate(moves):
+                if k:
+                    self.send(4 + i, src, dst, t.plane[k])
+                else:
+                    d = pltpu.make_async_copy(src, dst, self.ls.at[i])
+                    d.start()
+                    self.local.append(d)
+
+    def share(self):
+        t = self.t
+        self.arrived(4, self.dpu.at[t.c, :, pl.ds(0, 3)])
+        self.arrived(5, self.do.at[t.c, pl.ds(0, 144)])
+        self.arrived(6, self.dd.at[t.c, pl.ds(0, 3)])
+        for d in self.local:
+            d.wait()
+        for i, ref in enumerate((self.dpu, self.do, self.dd)):
+            view = ref.at[t.c, pl.ds(0, 192)] if i == 1 else ref.at[t.c]
+            self.send(7 + i, view, view, t.sib)
+
+    def finish(self):
+        for i, ref in enumerate((self.dpu, self.do, self.dd)):
+            view = ref.at[self.t.o, pl.ds(0, 192)] if i == 1 else ref.at[self.t.o]
+            self.arrived(7 + i, view)
+
+
+class Reduce(Sender):
+    def __init__(self, t, w, rc_, r1, r2, r3, fin, fin2, out, ss, rs):
+        super().__init__(t, ss, rs)
+        self.w, self.rc, self.r1, self.r2, self.r3 = w, rc_, r1, r2, r3
+        self.fin, self.fin2, self.out = fin, fin2, out
+
+    def pair(self):
+        self.send(0, self.w.at[self.t.o], self.rc, self.t.sib)
+
+    def add(self, q, part):
+        w, c = self.w, self.t.c
+
+        @pl.loop(0, 4)
+        def _(z):
+            w[c, z, q] = (w[c, z, q].astype(F32) + part[z].astype(F32)).astype(w.dtype)
+
+    def first(self):
+        t = self.t
+        self.arrived(0, self.rc)
+        for i, q in ((0, t.q2), (1, t.q12)):
+            self.add(q, self.rc.at[:, q])
+            self.send(1 + i, self.w.at[t.c, :, q], self.r1.at[i], t.n2)
+        for q in (t.q, t.q1):
+            self.add(q, self.rc.at[:, q])
+
+    def second(self):
+        t = self.t
+        self.arrived(2, self.r1.at[1])
+        self.add(t.q1, self.r1.at[1])
+        self.send(3, self.w.at[t.c, :, t.q1], self.r2, t.n1)
+        self.arrived(1, self.r1.at[0])
+        self.add(t.q, self.r1.at[0])
+
+    def third(self):
+        t = self.t
+        self.arrived(3, self.r2)
+        self.add(t.q, self.r2)
+        for k in range(3):
+            self.send(4, self.w.at[t.c, t.zz[k], t.q], self.r3.at[2 - k], t.zn[k])
+
+    def fourth(self):
+        t = self.t
+        self.arrived(4, self.r3)
+        total = self.w[t.c, t.z, t.q].astype(F32)
+        for k in range(3):
+            total = total + self.r3[k].astype(F32)
+        self.fin[...] = total
+        rd = self.fin.shape[0] // 2
+        self.send(5, self.fin.at[off(t.o, rd, 8)], self.fin2, t.sib)
+
+    def fifth(self):
+        t = self.t
+        rd, n2 = self.fin2.shape
+        self.arrived(5, self.fin2)
+        self.out[:, off(t.c, n2)] = self.fin[off(t.c, rd, 8), :]
+        self.out[:, off(t.o, n2)] = self.fin2[...]
+
+
+def dot(a, b):
+    return jnp.dot(a, b, preferred_element_type=F32)
+
+
+def dot_rt(a, b):
+    return lax.dot_general(a, b, (((1,), (1,)), ((), ())), preferred_element_type=F32)
+
+
+def dot_lt(a, b):
+    return lax.dot_general(a, b, (((0,), (0,)), ((), ())), preferred_element_type=F32)
+
+
+def normed(v):
+    centred = v - jnp.mean(v, axis=-1, keepdims=True)
+    inverse = lax.rsqrt(jnp.mean(centred * centred, axis=-1, keepdims=True) + epsilon)
+    return centred * inverse, inverse
+
+
+def norm_back(g, n, inverse, gain):
+    v = g * gain
+    return inverse * (
+        v - jnp.mean(v, axis=-1, keepdims=True) - n * jnp.mean(v * n, axis=-1, keepdims=True)
+    )
+
+
+def gelu_pair(v):
+    share = 0.5 * (1.0 + lax.erf(v * root_half))
+    return v * share, share + v * jnp.exp(-0.5 * v * v) * inverse_root_tau
+
+
+SIZES = ((24, 128, F32), (24, 1152, BF), (24, 384, BF), (24, 1536, BF), (96, 384, BF))
+WINDOWS = (
+    [((0, 48), (0, 128))],
+    [((0, 48), (384 * j, 384)) for j in range(3)],
+    [((0, 48), (0, 384))],
+    [((0, 48), (384 * j, 384)) for j in range(4)],
+    [((48 * j, 48), (0, 384)) for j in range(4)],
+)
+SCRATCH = {
+    "got": [((rd, n2), dt) for rd, n2, dt in SIZES] + [((24, 3456), BF), ((96, 384), BF)],
+    "w": [((2, 4, 4, 2 * rd, n2), dt) for rd, n2, dt in SIZES],
+    "fin": [((2 * rd, n2), F32) for rd, n2, dt in SIZES],
+    "fin2": [((rd, n2), F32) for rd, n2, dt in SIZES],
+    "rc": [((4, 4, 2 * rd, n2), dt) for rd, n2, dt in SIZES if n2 not in (1152, 384) or rd == 96],
+    "r1": [((2, 4, 2 * rd, n2), dt) for rd, n2, dt in SIZES],
+    "r2": [((4, 2 * rd, n2), dt) for rd, n2, dt in SIZES],
+    "r3": [((3, 2 * rd, n2), dt) for rd, n2, dt in SIZES],
+    "stage": [((4, 48, 3456), BF), ((4, 192, 384), BF)],
+    "dpu": [((2, 4, 4, 48, 768), BF)],
+    "do": [((2, 256, 384), BF)],
+    "dd": [((2, 4, 192, 384), BF)],
+    "vec": [((16, 768), F32)],
+    "table": [((16, 2, 768), F32)],
+    "pr": [((512, 2304), BF)],
+    "ctx": [((512, 768), BF)],
+    "sh": [((24, 256, 128), BF)],
+    "n1": [((512, 768), BF)],
+    "i1": [((512, 1), F32)],
+    "n2": [((512, 768), BF)],
+    "i2": [((512, 1), F32)],
+    "fl": [((512, 768), BF)],
+    "act": [((512, 3072), BF)],
+    "gp": [((512, 3072), BF)],
+    "row": [((512, 768), F32)],
+    "low": [((512, 768), BF)],
+    "ob": [((512, 768), BF)],
+    "hid": [((256, 384), F32)],
+    "src": [((2, 2, 768), F32)] * 2,
+    "slots": [((16, 2, 768), F32)] * 4,
+    "sdr": [((2, 4, 2, 768), F32)],
+    "pairs": [((2, 2, 768), F32)] * 2,
+    "soo": [((2, 768), F32)],
+    "mat": [((32, 768), F32)] * 2,
+    "ars": [((4, 32, 768), BF)],
+    "arb": [((4, 3, 32, 768), BF)],
+    "fq": [((2, 4, 4, 32, 1280), BF)],
+    "fz": [((2, 4, 32, 1536), BF)],
+    "vg": [((128, 768), F32)],
+    "flip": [((768, 128), F32)],
+}
+SEMS = {
+    "gs": (5, 4, 9),
+    "gr": (5, 4, 9),
+    "ds": (10,),
+    "dr": (10,),
+    "ls": (4,),
+    "rs": (5, 6),
+    "rr": (5, 6),
+    "xs": (12,),
+    "xr": (12,),
+    "fs": (2, 9),
+    "fr": (2, 9),
+    "os": (8,),
+}
+INS = ("tok", "cot", "tmask", "dmask", "small", "sp", "so", "su", "sd", "dmain", "ddown")
+OUTS = (
+    ("out", (512, 768), BF),
+    ("gin", (512, 768), F32),
+    ("gsmall", (24, 256), F32),
+    ("gsp", (24, 2304), F32),
+    ("gso", (24, 768), F32),
+    ("gsu", (24, 3072), F32),
+    ("gsd", (96, 768), F32),
+    ("gdp", (24, 3072), F32),
+    ("gdo", (24, 768), F32),
+    ("gdu", (24, 3072), F32),
+    ("gdd", (96, 768), F32),
+)
+
+
+class Box:
+    pass
+
+
+def kernel(*refs):
+    b = Box()
+    refs = list(refs)
+
+    def take(n):
+        got, refs[:n] = refs[:n], []
+        return got
+
+    for name in INS:
+        setattr(b, name, take(1)[0])
+    for name, _, _ in OUTS:
+        setattr(b, name, take(1)[0])
+    for name, items in SCRATCH.items():
+        got = take(len(items))
+        setattr(b, name, got if len(got) > 1 else got[0])
+    for name in SEMS:
+        setattr(b, name, take(1)[0])
+    b.credit = take(1)[0]
+    b.t = Spot()
+    run(b)
+
+
+def run(b):
+    t = b.t
+    b.x = Sender(t, b.xs, b.xr)
+    b.do[...] = jnp.zeros(b.do.shape, BF)
+    b.vg[...] = jnp.zeros(b.vg.shape, F32)
+    enter(t)
+    shards = (b.small, b.sp, b.so, b.su, b.sd)
+    gs = [
+        Gather(t, shards[i], b.w[i], b.got[i], b.fin[i], WINDOWS[i], b.gs.at[i], b.gr.at[i])
+        for i in range(5)
+    ]
+    dg = DocGather(
+        t, (b.dmain, b.ddown), b.stage, b.got[5:], (b.fin[1], b.fin[4]), b.dpu, b.do, b.dd, b.ds, b.dr, b.ls
+    )
+    for g in gs[:2]:
+        g.pair()
+    for g in gs[2:]:
+        g.pair()
+    dg.pair()
+    events = [(g, k) for g in gs for k in range(len(g.windows))]
+    clock = [0]
+
+    def do(name, at):
+        if 0 <= at < len(events):
+            getattr(events[at][0], name)(events[at][1])
+
+    def tick(upto):
+        while clock[0] <= upto:
+            at = clock[0]
+            do("first", at)
+            do("spread", at + 2)
+            if at + 2 == len(events):
+                dg.spread(0)
+                dg.spread(1)
+            do("second", at - 1)
+            do("third", at - 2)
+            do("finish", at - 3)
+            clock[0] += 1
+
+    gs[0].join()
+    gs[1].join()
+    do("spread", 0)
+    do("spread", 1)
+    for g in gs[2:]:
+        g.join()
+    dg.join()
+    send_cotangents(b)
+    tick(3)
+    vectors_in(b)
+    tick(6)
+    segment_project(b)
+    for seg in range(4):
+        attend(b, seg)
+        tick(7 + seg // 2)
+    segment_mix(b)
+    tick(9)
+    for j in range(4):
+        segment_up(b, j)
+        tick(10 + j)
+    tick(14)
+    dg.plane()
+    tick(15)
+    segment_down(b)
+    send_summaries(b)
+    dg.share()
+    for g in gs:
+        g.drain()
+    dg.finish()
+    dg.drain()
+    document(b)
+    finish_output(b)
+
+    small_rc, up_rc, down_rc = b.rc
+    rcs = (small_rc, up_rc.at[:, :, :, 0:1152], up_rc.at[:, :, :, 1152:1536], up_rc, down_rc)
+    rs = [
+        Reduce(t, b.w[i], rcs[i], b.r1[i], b.r2[i], b.r3[i], b.fin[i], b.fin2[i], out, b.rs.at[i], b.rr.at[i])
+        for i, out in enumerate((b.gsmall, b.gsp, b.gso, b.gsu, b.gsd))
+    ]
+    rsmall, rproject, routput, rup, rdown = rs
+    second_back(b)
+    hidden_back(b)
+    down_terms(b)
+    rdown.pair()
+    first_back(b)
+    rdown.first()
+    up_terms(b)
+    rup.pair()
+    mixed_back(b)
+    rdown.second()
+    output_terms(b)
+    rup.first()
+    pl.semaphore_signal(b.credit, inc=1, device_id=t.sib, device_id_type=MESH)
+    pl.semaphore_wait(b.credit, 1)
+    routput.pair()
+    rdown.third()
+    attend_back(b, 0)
+    attend_back(b, 1)
+    rup.second()
+    routput.first()
+    rdown.fourth()
+    attend_back(b, 2)
+    attend_back(b, 3)
+    project_terms(b)
+    rproject.pair()
+    rup.third()
+    routput.second()
+    rdown.fifth()
+    vectors_out(b)
+    rsmall.pair()
+    rproject.first()
+    routput.third()
+    rup.fourth()
+    document_terms(b)
+    rsmall.first()
+    rproject.second()
+    routput.fourth()
+    rup.fifth()
+    rsmall.second()
+    rproject.third()
+    routput.fifth()
+    rsmall.third()
+    rproject.fourth()
+    rsmall.fourth()
+    rproject.fifth()
+    rsmall.fifth()
+    for r in rs:
+        r.drain()
+    b.x.drain()
+    for d in b.flying:
+        d.wait()
+
+
+def send_cotangents(b):
+    for m in range(2):
+        for s in range(2):
+            rows = b.cot[pl.ds(128 * (2 * m + s), 16), :].astype(F32)
+            b.src[0][m, s : s + 1, :] = rows[0:1]
+    send_rows(b, 0)
+
+
+def send_rows(b, n):
+    t, src, slots = b.t, b.src[n], b.slots[n]
+    mine = src.at[t.half]
+    other = src.at[1 - t.half]
+    for k in (1, 2, 3):
+        b.x.send(n, mine, slots.at[t.i], t.plane[k])
+    for k in (0, 1, 2, 3):
+        b.x.send(n, mine, slots.at[t.i], (4 * t.z + t.qq[k], t.o))
+        b.x.send(n, other, slots.at[t.i], (4 * t.zo + t.qq[k], t.c))
+        b.x.send(n, other, slots.at[t.i], (4 * t.zo + t.qq[k], t.o))
+    slots[t.i] = src[t.half]
+
+
+def take_rows(b, n):
+    slots = b.slots[n]
+    b.x.arrived(n, slots.at[pl.ds(0, 15)])
+    for i in range(16):
+        b.mat[n][2 * i : 2 * i + 2, :] = slots[i]
+    return b.mat[n][...]
+
+
+def vectors_in(b):
+    small = b.w[0]
+    b.vec[...] = jnp.transpose(small[0].reshape(768, 128))[0:16]
+    table = jnp.transpose(small[1].reshape(768, 128))[0:32]
+    for i in range(16):
+        b.table[i] = table[2 * i : 2 * i + 2]
+
+
+def vec(b, i):
+    return b.vec[i : i + 1, :]
+
+
+def segment_project(b):
+    w = b.w[1]
+
+    @pl.loop(0, 6)
+    def _(i):
+        h, j = lax.div(i, 3), lax.rem(i, 3)
+        part = w[h, :, :, :, off(j, 384)].reshape(768, 384)
+        b.pr[:, off(i, 384)] = dot(b.tok[...], part).astype(BF)
+
+
+def lane_masks():
+    lane = lax.broadcasted_iota(jnp.int32, (1, 128), 1)
+    low = (lane < 64).astype(F32)
+    return low.astype(BF), (1.0 - low).astype(BF)
+
+
+def attend(b, seg):
+    low, high = lane_masks()
+    keep = b.tmask[seg : seg + 1, :] > 0.0
+    rows = pl.ds(128 * seg, 128)
+
+    @pl.loop(0, 6)
+    def _(p):
+        q2 = b.pr[rows, off(p, 128)]
+        k2 = b.pr[rows, off(p + 6, 128)]
+        v2 = b.pr[rows, off(p + 12, 128)]
+        qs = jnp.concatenate((q2 * low, q2 * high), axis=0)
+        scores = jnp.where(keep, dot_rt(qs, k2) * 0.125, floor_score)
+        raised = jnp.exp(scores - jnp.max(scores, axis=-1, keepdims=True))
+        shares = (raised * (1.0 / jnp.sum(raised, axis=-1, keepdims=True))).astype(BF)
+        b.sh[6 * seg + p] = shares
+        both = dot(shares, v2)
+        lane = lax.broadcasted_iota(jnp.int32, (128, 128), 1)
+        b.ctx[rows, off(p, 128)] = jnp.where(lane < 64, both[:128], both[128:]).astype(BF)
+
+
+def segment_mix(b):
+    w = b.w[2]
+    for r in range(2):
+        rows = pl.ds(256 * r, 256)
+        for h in range(2):
+            b.row[rows, pl.ds(384 * h, 384)] = dot(b.ctx[rows, :], w[h].reshape(768, 384))
+    scale, offset = vec(b, 0), vec(b, 1)
+
+    @pl.loop(0, 16)
+    def _(i):
+        rows = off(i, 32, 32)
+        n, inverse = normed(b.tok[rows, :].astype(F32) + b.row[rows, :])
+        first = n * scale + offset
+        b.n1[rows, :] = n.astype(BF)
+        b.i1[rows, :] = inverse
+        b.row[rows, :] = first
+        b.fl[rows, :] = first.astype(BF)
+
+
+def segment_up(b, j):
+    w = b.w[3]
+    for h, r in ((0, 0), (0, 1), (1, 0), (1, 1)):
+        up = w[h, :, :, :, pl.ds(384 * j, 384)].reshape(768, 384)
+        b.hid[...] = dot(b.fl[256 * r : 256 * r + 256, :], up)
+        cols = pl.ds(1536 * h + 384 * j, 384)
+
+        @pl.loop(0, 8)
+        def _(i):
+            rows = off(i + 8 * r, 32, 32)
+            value, slope = gelu_pair(b.hid[off(i, 32, 32), :])
+            b.act[rows, cols] = value.astype(BF)
+            b.gp[rows, cols] = slope.astype(BF)
+
+
+def segment_down(b):
+    w = b.w[4]
+
+    @pl.loop(0, 4)
+    def _(i):
+        h, r = lax.div(i, 2), lax.rem(i, 2)
+        rows = off(r, 256, 256)
+        b.row[rows, off(h, 384)] += dot(b.act[rows, :], w[h].reshape(3072, 384))
+
+    gain, shift = vec(b, 2), vec(b, 3)
+
+    @pl.loop(0, 16)
+    def _(i):
+        rows = off(i, 32, 32)
+        n, inverse = normed(b.row[rows, :])
+        b.n2[rows, :] = n.astype(BF)
+        b.i2[rows, :] = inverse
+        second = n * gain + shift
+        b.row[rows, :] = second
+        b.ob[rows, :] = second.astype(BF)
+
+
+def send_summaries(b):
+    t = b.t
+    places = b.table[t.i]
+    for m in range(2):
+        for s in range(2):
+            rows = b.row[pl.ds(128 * (2 * m + s), 8), :]
+            b.src[1][m, s : s + 1, :] = rows[0:1] + places[s : s + 1]
+    send_rows(b, 1)
+
+
+def plane_sum(b, n, partial):
+    t = b.t
+    b.ars[n] = partial.astype(BF)
+    for k in (1, 2, 3):
+        b.x.send(2 + n, b.ars.at[n], b.arb.at[n, k - 1], t.plane[k])
+    b.x.arrived(2 + n, b.arb.at[n])
+    total = b.ars[n].astype(F32)
+    for k in range(3):
+        total = total + b.arb[n, k].astype(F32)
+    return total
+
+
+def document(b):
+    t = b.t
+    dp = b.dpu[0].reshape(768, 768)
+    du = b.dpu[1].reshape(768, 768)
+    lane = lax.broadcasted_iota(jnp.int32, (1, 256), 1)
+    heads = [((lane >= 64 * h) & (lane < 64 * h + 64)).astype(F32).astype(BF) for h in range(3)]
+    keep = b.dmask[...] > 0.0
+    h_in = take_rows(b, 1)
+    h_low = h_in.astype(BF)
+    pr = dot(h_low, dp).astype(BF)
+    q3, k3, v3 = pr[:, 0:256], pr[:, 256:512], pr[:, 512:768]
+    qs = jnp.concatenate([q3 * m for m in heads], axis=0)
+    scores = jnp.where(keep, dot_rt(qs, k3) * 0.125, floor_score)
+    raised = jnp.exp(scores - jnp.max(scores, axis=-1, keepdims=True))
+    shares = raised * (1.0 / jnp.sum(raised, axis=-1, keepdims=True))
+    shares_low = shares.astype(BF)
+    three = dot(shares_low, v3)
+    ctx = sum(three[32 * h : 32 * h + 32] * heads[h].astype(F32) for h in range(3)).astype(BF)
+    mixed = jnp.concatenate([dot(ctx, b.do[h]) for h in range(2)], axis=1)
+    n1, i1 = normed(h_in + plane_sum(b, 0, mixed))
+    first = n1 * vec(b, 4) + vec(b, 5)
+    first_low = first.astype(BF)
+    active, slope = gelu_pair(dot(first_low, du))
+    active = active.astype(BF)
+    branch = jnp.concatenate([dot(active, b.dd[h].reshape(768, 384)) for h in range(2)], axis=1)
+    n2, i2 = normed(first + plane_sum(b, 1, branch))
+    out = n2 * vec(b, 6) + vec(b, 7)
+    for i in range(16):
+        b.slots[2][i] = out[2 * i : 2 * i + 2]
+    other_i = 8 * (1 - t.half) + 2 * t.q + t.c
+    b.x.send(6, b.slots[2].at[other_i], b.soo, (4 * t.zo + t.q, t.c))
+
+    g = take_rows(b, 0)
+    b.vg[6:7, :] = jnp.sum(g * n2, axis=0, keepdims=True) * 0.125
+    b.vg[7:8, :] = jnp.sum(g, axis=0, keepdims=True) * 0.125
+    delta = norm_back(g, n2, i2, vec(b, 6))
+    branch_low = delta.astype(BF)
+    back = sum(dot_rt(branch_low[:, 384 * h : 384 * h + 384], b.dd[h].reshape(768, 384)) for h in range(2))
+    hidden_delta = (back * slope).astype(BF)
+    first_delta = delta + plane_sum(b, 2, dot_rt(hidden_delta, du))
+    b.vg[4:5, :] = jnp.sum(first_delta * n1, axis=0, keepdims=True) * 0.125
+    b.vg[5:6, :] = jnp.sum(first_delta, axis=0, keepdims=True) * 0.125
+    mixed_delta = norm_back(first_delta, n1, i1, vec(b, 4))
+    mixed_low = mixed_delta.astype(BF)
+    ctx_delta = sum(dot_rt(mixed_low[:, 384 * h : 384 * h + 384], b.do[h]) for h in range(2)).astype(BF)
+    cs = jnp.concatenate([ctx_delta * m for m in heads], axis=0)
+    shares_delta = dot_rt(cs, v3)
+    inner = jnp.sum(shares_delta * shares, axis=-1, keepdims=True)
+    scores_delta = (shares * (shares_delta - inner)).astype(BF)
+    dq3 = dot(scores_delta, k3) * 0.125
+    dq = sum(dq3[32 * h : 32 * h + 32] * heads[h].astype(F32) for h in range(3))
+    dk = dot_lt(scores_delta, qs) * 0.125
+    dv = dot_lt(shares_low, cs)
+    pd = jnp.concatenate((dq, dk, dv), axis=1).astype(BF)
+    h_delta = dot_rt(pd, dp) + 0.25 * mixed_delta
+    for i in range(16):
+        b.slots[3][i] = h_delta[2 * i : 2 * i + 2]
+    for k in (0, 1, 2, 3):
+        if k:
+            b.x.send(7, b.slots[3].at[8 * t.half + 2 * t.qq[k] + t.c], b.sdr.at[0, k], t.plane[k])
+        b.x.send(
+            8, b.slots[3].at[8 * (1 - t.half) + 2 * t.qq[k] + t.c], b.sdr.at[1, k], (4 * t.zo + t.qq[k], t.c)
+        )
+    b.sdr[0, 0] = b.slots[3][t.i]
+
+    @pl.when(t.c == 0)
+    def _():
+        b.fq[0, t.z, t.q, :, 0:768] = pd
+        b.fq[0, t.z, t.q, :, 768:1024] = ctx
+        b.fq[0, t.z, t.q, :, 1024:1280] = active[:, 0:256]
+        b.fz[0, t.z, :, 0:768] = h_low
+        b.fz[0, t.z, :, 768:1536] = mixed_low
+
+    @pl.when(t.c == 1)
+    def _():
+        b.fq[1, t.z, t.q, :, 0:768] = hidden_delta
+        b.fq[1, t.z, t.q, :, 768:1280] = active[:, 256:768]
+        b.fz[1, t.z, :, 0:768] = first_low
+        b.fz[1, t.z, :, 768:1536] = branch_low
+
+    b.f = Gather(t, None, b.fq, None, None, [((0, 32), (0, 1280))], b.fs, b.fr)
+    b.f.spread(0)
+    for dev in t.zn:
+        b.f.send((1, 0), b.fz.at[t.c, t.z], b.fz.at[t.c, t.z], dev)
+    b.x.arrived(6, b.soo)
+    b.pairs[0][t.half] = b.slots[2][t.i]
+    b.pairs[0][1 - t.half] = b.soo[...]
+    b.x.arrived(7, b.sdr.at[0, pl.ds(0, 3)])
+    b.x.arrived(8, b.sdr.at[1])
+    b.pairs[1][t.half] = b.sdr[0, 0] + b.sdr[0, 1] + b.sdr[0, 2] + b.sdr[0, 3]
+    b.pairs[1][1 - t.half] = b.sdr[1, 0] + b.sdr[1, 1] + b.sdr[1, 2] + b.sdr[1, 3]
+    b.f.first(0)
+    b.f.arrived((1, 0), b.fz.at[t.c, pl.ds(0, 3)])
+    b.f.send((1, 1), b.fz.at[t.c], b.fz.at[t.c], t.sib)
+    b.f.second(0)
+
+
+def finish_output(b):
+    first_row = lax.broadcasted_iota(jnp.int32, (16, 768), 0) == 0
+    for m in range(2):
+        for s in range(2):
+            rows = pl.ds(128 * (2 * m + s), 16)
+            fresh = jnp.where(first_row, b.pairs[0][m, s : s + 1, :], b.ob[rows, :].astype(F32))
+            b.ob[rows, :] = fresh.astype(BF)
+    d = pltpu.make_async_copy(b.ob, b.out, b.os.at[0])
+    d.start()
+    b.flying = [d]
+
+
+def second_back(b):
+    gain = vec(b, 2)
+
+    def body(i, carry):
+        gains, shifts = carry
+        rows = off(i, 16, 16)
+        seg = lax.div(i, 8)
+        fresh = (lax.broadcasted_iota(jnp.int32, (16, 768), 0) + 16 * lax.rem(i, 8)) == 0
+        own = b.pairs[1][lax.div(seg, 2)]
+        own = jnp.where(lax.rem(seg, 2) == 0, own[0:1], own[1:2])
+        g = jnp.where(fresh, own, b.cot[rows, :].astype(F32))
+        n = b.n2[rows, :].astype(F32)
+        delta = norm_back(g, n, b.i2[rows, :], gain)
+        b.row[rows, :] = delta
+        b.low[rows, :] = delta.astype(BF)
+        return gains + g * n, shifts + g
+
+    zero = jnp.zeros((16, 768), F32)
+    gains, shifts = lax.fori_loop(0, 32, body, (zero, zero))
+    b.vg[2:3, :] = jnp.sum(gains, axis=0, keepdims=True)
+    b.vg[3:4, :] = jnp.sum(shifts, axis=0, keepdims=True)
+
+
+def hidden_back(b):
+    w = b.w[4]
+
+    @pl.loop(0, 4)
+    def _(z):
+        cols = off(z, 768)
+        for r in range(2):
+            rows = pl.ds(256 * r, 256)
+            back = dot_rt(b.low[rows, 0:384], w[0, z].reshape(768, 384)) + dot_rt(
+                b.low[rows, 384:768], w[1, z].reshape(768, 384)
+            )
+            b.gp[rows, cols] = (back * b.gp[rows, cols].astype(F32)).astype(BF)
+
+
+def down_terms(b):
+    w = b.w[4]
+
+    @pl.loop(0, 4)
+    def _(z):
+        a = b.act[:, off(z, 768)]
+        for h in range(2):
+            w[h, z] = dot_lt(a, b.low[:, 384 * h : 384 * h + 384]).astype(BF).reshape(4, 192, 384)
+
+
+def first_back(b):
+    w = b.w[3]
+
+    @pl.loop(0, 2)
+    def _(r):
+        rows = off(r, 256, 256)
+        for h in range(2):
+            b.row[rows, :] += dot_rt(b.gp[rows, 1536 * h : 1536 * h + 1536], w[h].reshape(768, 1536))
+
+
+def up_terms(b):
+    w = b.w[3]
+
+    @pl.loop(0, 8)
+    def _(i):
+        h, j = lax.div(i, 4), lax.rem(i, 4)
+        part = dot_lt(b.fl[...], b.gp[:, off(i, 384)])
+        w[h, :, :, :, off(j, 384)] = part.astype(BF).reshape(4, 4, 48, 384)
+
+
+def mixed_back(b):
+    scale = vec(b, 0)
+
+    def body(i, carry):
+        scales, offsets = carry
+        rows = off(i, 16, 16)
+        g = b.row[rows, :]
+        n = b.n1[rows, :].astype(F32)
+        delta = norm_back(g, n, b.i1[rows, :], scale)
+        b.row[rows, :] = delta
+        b.low[rows, :] = delta.astype(BF)
+        return scales + g * n, offsets + g
+
+    zero = jnp.zeros((16, 768), F32)
+    scales, offsets = lax.fori_loop(0, 32, body, (zero, zero))
+    b.vg[0:1, :] = jnp.sum(scales, axis=0, keepdims=True)
+    b.vg[1:2, :] = jnp.sum(offsets, axis=0, keepdims=True)
+
+
+def output_terms(b):
+    w = b.w[2]
+    b.flying[0].wait()
+    b.flying = []
+    for r in range(2):
+        rows = pl.ds(256 * r, 256)
+        back = dot_rt(b.low[rows, 0:384], w[0].reshape(768, 384)) + dot_rt(
+            b.low[rows, 384:768], w[1].reshape(768, 384)
+        )
+        b.ob[rows, :] = back.astype(BF)
+    for h in range(2):
+        w[h] = dot_lt(b.ctx[...], b.low[:, 384 * h : 384 * h + 384]).astype(BF).reshape(4, 4, 48, 384)
+
+
+def attend_back(b, seg):
+    low, high = lane_masks()
+    rows = pl.ds(128 * seg, 128)
+
+    @pl.loop(0, 6)
+    def _(p):
+        q2 = b.pr[rows, off(p, 128)]
+        k2 = b.pr[rows, off(p + 6, 128)]
+        v2 = b.pr[rows, off(p + 12, 128)]
+        d2 = b.ob[rows, off(p, 128)]
+        qs = jnp.concatenate((q2 * low, q2 * high), axis=0)
+        cs = jnp.concatenate((d2 * low, d2 * high), axis=0)
+        shares_low = b.sh[6 * seg + p]
+        shares = shares_low.astype(F32)
+        shares_delta = dot_rt(cs, v2)
+        inner = jnp.sum(shares_delta * shares, axis=-1, keepdims=True)
+        scores_delta = (shares * (shares_delta - inner)).astype(BF)
+        dq = dot(scores_delta, k2) * 0.125
+        lane = lax.broadcasted_iota(jnp.int32, (128, 128), 1)
+        b.pr[rows, off(p, 128)] = jnp.where(lane < 64, dq[:128], dq[128:]).astype(BF)
+        b.pr[rows, off(p + 6, 128)] = (dot_lt(scores_delta, qs) * 0.125).astype(BF)
+        b.pr[rows, off(p + 12, 128)] = dot_lt(shares_low, cs).astype(BF)
+
+
+def project_terms(b):
+    w = b.w[1]
+
+    @pl.loop(0, 2)
+    def _(r):
+        rows = off(r, 256, 256)
+        for h in range(2):
+            b.row[rows, :] += dot_rt(b.pr[rows, 1152 * h : 1152 * h + 1152], w[h].reshape(768, 1152))
+
+    d = pltpu.make_async_copy(b.row, b.gin, b.os.at[1])
+    d.start()
+    b.flying = [d]
+
+    @pl.loop(0, 6)
+    def _(i):
+        h, j = lax.div(i, 3), lax.rem(i, 3)
+        part = dot_lt(b.tok[...], b.pr[:, off(i, 384)])
+        w[h, :, :, :, off(j, 384)] = part.astype(BF).reshape(4, 4, 48, 384)
+
+
+def vectors_out(b):
+    t, w = b.t, b.w[0]
+    w[0] = jnp.transpose(b.vg[...]).reshape(4, 4, 48, 128)
+    row = lax.broadcasted_iota(jnp.int32, (32, 768), 0)
+    both = b.pairs[1][0] + b.pairs[1][1]
+    places = jnp.where(row == 2 * t.i, both[0:1], 0.0) + jnp.where(row == 2 * t.i + 1, both[1:2], 0.0)
+    b.vg[0:32, :] = places
+    w[1] = jnp.transpose(b.vg[...]).reshape(4, 4, 48, 128)
+
+
+def document_terms(b):
+    t = b.t
+    b.f.third(0)
+    b.f.finish(0)
+    b.f.arrived((1, 1), b.fz.at[t.o])
+    b.f.drain()
+    own = 24 * t.dev
+    part = 24 * lax.rem(t.dev, 8)
+
+    def rows_of(value, at, size):
+        n = value.shape[1]
+        b.flip[0:n, :] = jnp.transpose(value.astype(F32))
+        return b.flip[pl.ds(pl.multiple_of(at, 8), size), :].astype(BF)
+
+    left = rows_of(b.fz[0, :, :, 0:768].reshape(128, 768), own, 24)
+    for q in range(4):
+        b.gdp[:, 768 * q : 768 * q + 768] = dot(left, b.fq[0, :, q, :, 0:768].reshape(128, 768))
+    left = rows_of(b.fq[0, :, t.z, :, 768:1024].reshape(128, 256), part, 24)
+    b.gdo[...] = dot(left, b.fz[0, :, :, 768:1536].reshape(128, 768))
+    left = rows_of(b.fz[1, :, :, 0:768].reshape(128, 768), own, 24)
+    for q in range(4):
+        b.gdu[:, 768 * q : 768 * q + 768] = dot(left, b.fq[1, :, q, :, 0:768].reshape(128, 768))
+    active = jnp.concatenate((b.fq[0, :, t.z, :, 1024:1280], b.fq[1, :, t.z, :, 768:1280]), axis=-1)
+    left = rows_of(active.reshape(128, 768), 4 * part, 96)
+    b.gdd[...] = dot(left, b.fz[1, :, :, 768:1536].reshape(128, 768))
+
+
+def mega(*arrays):
+    vm = pl.BlockSpec(memory_space=pltpu.VMEM)
+    an = pl.BlockSpec(memory_space=pl.ANY)
+    return pl.pallas_call(
+        kernel,
+        out_shape=[jax.ShapeDtypeStruct(shape, dt) for _, shape, dt in OUTS],
+        in_specs=[vm] * len(INS),
+        out_specs=[an, an] + [vm] * (len(OUTS) - 2),
+        scratch_shapes=[pltpu.VMEM(shape, dt) for items in SCRATCH.values() for shape, dt in items]
+        + [pltpu.SemaphoreType.DMA(shape) for shape in SEMS.values()]
+        + [pltpu.SemaphoreType.REGULAR],
+        compiler_params=pltpu.CompilerParams(
+            collective_id=1, has_side_effects=True, vmem_limit_bytes=65200 * 1024
+        ),
+    )(*arrays)
+
+
+def local_fast(tokens, token_counts, *rest):
+    weights, cotangent = rest[:17], rest[17]
+    batches, segments, length, width = tokens.shape
+    device = lax.axis_index("seg") * 2 + lax.axis_index("rep")
+    own = lax.dynamic_slice(token_counts, (0, device * segments), (batches, segments)).reshape(-1)
+    slots = jnp.arange(length)
+    tmask = ((slots[None] < own[:, None]) | (slots[None] == 0)).astype(F32)
+    z = lax.div(lax.axis_index("seg"), 4)
+    doc = lax.dynamic_slice(
+        token_counts, (lax.rem(z, 2), lax.div(z, 2) * DOC_SEGS), (1, DOC_SEGS)
+    )
+    dmask = (doc > 0).astype(F32)
+    rows = weights[0].shape[0]
+    vectors = jnp.stack([weights[i] for i in (4, 5, 6, 7, 12, 13, 14, 15)], axis=1)
+    small = jnp.concatenate(
+        (
+            vectors,
+            jnp.zeros((rows, 120), BF),
+            weights[16],
+            jnp.zeros((rows, 96), BF),
+        ),
+        axis=1,
+    ).astype(F32)
+    project = jnp.pad(weights[8].reshape(rows, 3, 4, 192), ((0, 0), (0, 0), (0, 0), (0, 64)))
+    project = jnp.transpose(project, (0, 2, 1, 3)).reshape(rows, 3072)
+    dmain = jnp.concatenate((project, weights[9][:, :384], weights[10], weights[9][:, 384:]), axis=1)
+    outs = mega(
+        tokens.reshape(-1, width),
+        cotangent.reshape(-1, width),
+        tmask,
+        dmask,
+        small,
+        *weights[:4],
+        dmain,
+        weights[11],
+    )
+    out, gin, gsmall, gsp, gso, gsu, gsd, gdp, gdo, gdu, gdd = outs
+    gdp = gdp.reshape(rows, 4, 3, 256)[:, :, :, :192]
+    gdp = jnp.transpose(gdp, (0, 2, 1, 3)).reshape(rows, 2304)
+    return (
+        (out.reshape(tokens.shape), gin.reshape(tokens.shape), gsp, gso, gsu, gsd)
+        + tuple(gsmall[:, i] for i in range(4))
+        + (gdp, gdo, gdu, gdd)
+        + tuple(gsmall[:, i] for i in range(4, 8))
+        + (gsmall[:, 128:160],)
+    )
 
 
 def partner_2(value, axis, distance):
@@ -482,8 +1510,10 @@
 
 
 def solution(mesh):
+    sizes = dict(mesh.shape)
+    body = local_fast if (sizes["seg"], sizes["rep"]) == (16, 2) else local
     return jax.shard_map(
-        local,
+        body,
         mesh=mesh,
         in_specs=(
             P(None, ("seg", "rep"), None, None),

time: 1430 us -> 320 us (0.22)
  waiting for transfers between devices: 720 us -> 0 us
  Pallas kernels: 0 us -> 293 us
  blocking collectives: 182 us -> 0 us
  matrix products: 154 us -> 0 us
  starting transfers between devices: 152 us -> 0 us
  local copies, waits for them, and re-layouts: 105 us -> 22 us
  other arithmetic: 83.3 us -> 3.32 us
  between operations: 18.2 us -> 0.81 us
    all_to_all x16 -> x0, waiting for transfers between devices: 400 us -> none  [the longest x1 82.1 us: local(): lax.all_to_all(shaped[11].astype(jnp.bfloat16), 'seg', split_axis=0, conc...]
    all_gather x8 -> x0, waiting for transfers between devices: 301 us -> none  [the longest x1 61.7 us: local(): lax.all_gather(document_down, ('seg', 'rep'), axis=0, tiled=True)]
    pallas_call x0 -> x1, Pallas kernels: none -> 293 us  [mega(): pl.pallas_call(kernel, out_shape=[jax.ShapeDtypeStruct(shape, dt) for _,...]
    dot_general x72 -> x0, matrix products: 154 us -> none  [the longest x16 44.5 us: left_product(): lax.dot_general(left, right, (((0,), (0,)), ((), ())), preferred_element_...]
    all_to_all x16 -> x0, starting transfers between devices: 135 us -> none  [the longest x1 22.7 us: local(): lax.all_to_all(shaped[2].astype(jnp.bfloat16), 'seg', split_axis=0, conca...]
    all_to_all x1 -> x0, blocking collectives: 94.5 us -> none  [local(): lax.all_to_all(shaped[0].astype(jnp.bfloat16), 'seg', split_axis=0, conca...]
    unnamed x2 -> x0, blocking collectives: 46.3 us -> none
    all_gather x1 -> x0, blocking collectives: 41.3 us -> none  [local(): lax.all_gather(position, ('seg', 'rep'), axis=0, tiled=True)]
  transfers between devices with their start and end apart: 49 -> 0, of which waited for: 30 -> 0; matrix products, arithmetic and copies ran while one was open for 19% -> 0% of each run, Pallas kernels for 0% -> 0%
where the time goes in v1:
time: 320 us
  Pallas kernels  293 us (92%)
  local copies, waits for them, and re-layouts  22 us (7%)
  other arithmetic  3.32 us (1%)
    pallas_call x1, Pallas kernels, mega(): pl.pallas_call(kernel, out_shape=[jax.ShapeDtypeStruct(shape, dt) for _,...  293 us
    unnamed x29, local copies, waits for them, and re-layouts  6.87 us

profile of v1, /device:TPU:1, one launch (start us, length us, event | category | flops | bytes accessed | tf_op | source)
XLA Modules:
  0.0 319.5 jit_solution(12257938851827772782)
XLA Ops:
  0.7 1.3 compare_convert_fusion.refs_3_
  2.0 0.7 constant_dynamic-slice_fusion
  2.8 0.7 fusion.1.refs_2_
  3.5 0.7 copy.58
  4.2 0.7 copy.59
  5.0 0.7 copy.60
  5.7 0.7 copy.61
  6.5 0.7 copy.62
  7.2 0.7 copy.63
  8.0 0.7 copy.64
  8.7 0.7 copy.65
  9.5 0.8 concatenate.6
  10.3 0.6 convert_element_type.13.refs_4_
  10.9 0.7 fusion.2
  11.6 1.1 reshape.70
  12.8 0.1 pad_bitcast_fusion
  12.9 0.2 reshape.71
  13.1 0.8 pad_maximum_fusion.refs_9_
  13.8 293.4 %shard_map.339 = (bf16[512,768]{1,0:T(8,128)(2,1)}, f32[512,768]{1,0:T(8,128)}, f32[24,256]{1,0:T(8,128)}, f32[24,2304]{1,0:T(8,128)}, f32[24,768]{1,0:T(8,128)}...) custom-call(bf16[512,768]{1,0:T(8,128)(2,1)} %bitcast.18, ...), custom_call_target="tpu_custom_call" | custom-call | tf_op jit(solution)/shard_map/pallas_call | solution.py:984
  307.3 1.8 slice_reduce_fusion
  309.1 1.3 slice.47
  310.4 1.2 reshape.74
  311.7 0.9 reshape.75
  312.6 0.9 copy.77
  313.5 1.1 copy.78
  314.7 0.7 copy.79
  315.4 0.6 copy.80
  316.0 0.7 copy.81
  316.7 0.7 copy.82
  317.4 0.6 copy.83
  318.1 0.7 copy.84
  318.8 0.7 copy.85
  (27 shorter events, 0.4 us)
Async XLA Ops:
  0.7 12.4 %copy-start.7 = (bf16[24,3072]{1,0:T(8,128)(2,1)S(1)}, bf16[24,3072]{1,0:T(8,128)(2,1)}, u32[]{:S(2)}) copy-start(bf16[24,3072]{1,0:T(8,128)(2,1)} %param.32) | copy-start | bytes 442372
  307.2 5.4 %copy-start.1 = (bf16[512,768]{1,0:T(8,128)(2,1)S(1)}, bf16[512,768]{1,0:T(8,128)(2,1)}, u32[]{:S(2)}) copy-start(bf16[512,768]{1,0:T(8,128)(2,1)} %get-tuple-element.30) | copy-start | bytes 2359300
  311.6 1.9 copy-start
  313.5 1.2 copy-start.6
  313.5 1.9 copy-start.9
  313.5 2.5 copy-start.5
  313.5 3.2 %copy-start.4 = (f32[96,768]{1,0:T(8,128)S(1)}, f32[96,768]{1,0:T(8,128)}, u32[]{:S(2)}) copy-start(f32[96,768]{1,0:T(8,128)} %get-tuple-element.75) | copy-start | bytes 884740
  314.7 2.8 copy-start.8
  314.7 3.4 %copy-start.3 = (f32[24,3072]{1,0:T(8,128)S(1)}, f32[24,3072]{1,0:T(8,128)}, u32[]{:S(2)}) copy-start(f32[24,3072]{1,0:T(8,128)} %get-tuple-element.82) | copy-start | bytes 884740
  314.7 4.1 %copy-start.2 = (f32[96,768]{1,0:T(8,128)S(1)}, f32[96,768]{1,0:T(8,128)}, u32[]{:S(2)}) copy-start(f32[96,768]{1,0:T(8,128)} %get-tuple-element.83) | copy-start | bytes 884740

commit v2 on v1

--- a/solution.py
+++ b/solution.py
@@ -32,7 +32,17 @@
         self.sib = (s, 1 - c)
         self.n1 = (4 * z + self.q1, c)
         self.n2 = (4 * z + self.q2, c)
+        self.diagonal = (4 * z + self.q12, c)
         self.zz = [lax.rem(z + k, 4) for k in (1, 2, 3)]
+        odd, high = lax.rem(z, 2), lax.div(z, 2)
+        self.middle = (z == 1) | (z == 2)
+        self.end = (z == 0) | (z == 3)
+        self.zs = [
+            (4 * (1 + odd) + self.q, c),
+            (4 * ((1 - odd) * (2 + high) + odd * high) + self.q, c),
+        ]
+        self.pass_from = jnp.where(z == 1, 2, 0)
+        self.tip = (4 * jnp.where(z == 2, 3, 0) + self.q, c)
         self.zn = [(4 * zz + self.q, c) for zz in self.zz]
         self.qq = [lax.rem(self.q + k, 4) for k in (0, 1, 2, 3)]
         self.plane = [(4 * z + qq, c) for qq in self.qq]
@@ -50,15 +60,15 @@
 
 def enter(t):
     bar = pltpu.get_barrier_semaphore()
-    everyone = [t.sib]
-    for k in range(4):
-        for e in range(4):
-            if k or e:
-                s = 4 * lax.rem(t.z + k, 4) + lax.rem(t.q + e, 4)
-                everyone += [(s, t.c), (s, t.o)]
+    everyone = [t.sib, t.n1, t.n2, t.diagonal] + t.zn
     for dev in everyone:
         pl.semaphore_signal(bar, inc=1, device_id=dev, device_id_type=MESH)
     pl.semaphore_wait(bar, len(everyone))
+
+
+def pass_on(t, sem):
+    for dev in (t.sib, t.n1, t.n2, t.diagonal):
+        pl.semaphore_signal(sem, inc=1, device_id=dev, device_id_type=MESH)
 
 
 class Sender:
@@ -73,10 +83,41 @@
     def arrived(self, at, ref):
         remote(ref, ref, self.ss.at[at], self.rs.at[at], self.t.sib).wait_recv()
 
+    def send_when(self, cond, at, src, dst, dev):
+        d = remote(src, dst, self.ss.at[at], self.rs.at[at], dev)
+        pl.when(cond)(d.start)
+        self.pending.append((cond, d))
+
     def drain(self):
         for d in self.pending:
-            d.wait_send()
+            if isinstance(d, tuple):
+                pl.when(d[0])(d[1].wait_send)
+            else:
+                d.wait_send()
         self.pending = []
+
+    def z_spread(self, at, view):
+        t = self.t
+        for dev in t.zs:
+            self.send(at, view(t.z), view(t.z), dev)
+
+    def z_relay(self, at, at2, view):
+        t = self.t
+        two = view(pl.ds(t.pass_from, 2))
+        d = remote(two, two, self.ss.at[at2], self.rs.at[at2], t.tip)
+
+        @pl.when(t.middle)
+        def _():
+            self.arrived(at, view(pl.ds(0, 3)))
+            d.start()
+
+        self.pending.append((t.middle, d))
+
+    def z_last(self, at, at2, view):
+        @pl.when(self.t.end)
+        def _():
+            self.arrived(at, view(0))
+            self.arrived(at2, view(pl.ds(0, 2)))
 
 
 def off(at, size, step=128):
@@ -94,13 +135,13 @@
 
 
 class Gather(Sender):
-    def __init__(self, t, shard, w, got, tmp, windows, ss, rs):
+    def __init__(self, t, far, shard, w, got, tmp, windows, ss, rs):
         super().__init__(t, ss, rs)
-        self.shard, self.w, self.got, self.tmp, self.windows = shard, w, got, tmp, windows
+        self.far, self.shard, self.w, self.got, self.tmp, self.windows = far, shard, w, got, tmp, windows
 
     def pair(self):
         n2 = self.got.shape[1]
-        self.send((0, 0), self.shard.at[:, off(self.t.o, n2)], self.got, self.t.sib)
+        self.send((0, 0), self.far.at[:, off(self.t.o, n2)], self.got, self.t.sib)
 
     def join(self):
         t = self.t
@@ -114,15 +155,18 @@
     def line(self, k, q):
         return self.pick(k, slice(None), q)
 
+    def view(self, k):
+        return lambda at: self.pick(k, at, self.t.q)
+
     def spread(self, k):
-        t = self.t
-        own = self.pick(k, t.z, t.q)
-        for dev in t.zn:
-            self.send((k, 1), own, own, dev)
+        self.z_spread((k, 1), self.view(k))
+
+    def relay(self, k):
+        self.z_relay((k, 1), (k, 9), self.view(k))
 
     def first(self, k):
         t = self.t
-        self.arrived((k, 1), self.pick(k, pl.ds(0, 3), t.q))
+        self.z_last((k, 1), (k, 9), self.view(k))
         line = self.line(k, t.q)
         self.send((k, 2), line, line, t.n1)
         self.send((k, 4), line, line, t.sib)
@@ -147,120 +191,200 @@
             self.arrived((k, i), self.line(k, self.t.q))
 
 
+class LineGather(Sender):
+    def __init__(self, t, w, windows, ss, rs):
+        super().__init__(t, ss, rs)
+        self.w, self.windows = w, windows
+
+    def view(self, k):
+        cols = self.windows[k]
+        return lambda at: self.w.at[self.t.c, at, :, pl.ds(*cols)]
+
+    def spread(self, k):
+        self.z_spread((k, 0), self.view(k))
+
+    def relay(self, k):
+        self.z_relay((k, 0), (k, 1), self.view(k))
+
+    def first(self, k):
+        self.z_last((k, 0), (k, 1), self.view(k))
+        line = self.view(k)(slice(None))
+        self.send((k, 2), line, line, self.t.sib)
+
+    def finish(self, k):
+        self.arrived((k, 2), self.view(k)(slice(None)))
+
+
 class DocGather(Sender):
-    def __init__(self, t, shards, stages, gots, tmps, dpu, do, dd, ss, rs, ls):
+    def __init__(self, t, far, shards, stages, gots, tmps, dpu, do, dd, ss, rs, ls):
         super().__init__(t, ss, rs)
-        self.shards, self.stages, self.gots, self.tmps = shards, stages, gots, tmps
+        self.far, self.shards, self.stages, self.gots, self.tmps = far, shards, stages, gots, tmps
         self.dpu, self.do, self.dd, self.ls = dpu, do, dd, ls
+        main, down = stages
+        q = t.qq
+        self.views = [(lambda at, k=k: main.at[at, :, off(q[k], 768)]) for k in (1, 2, 3, 0)]
+        self.views.append(lambda at: main.at[at, :, pl.ds(3072, 384)])
+        self.views += [(lambda at, j=j: down.at[at, pl.ds(96 * j, 96)]) for j in range(2)]
 
     def pair(self):
-        for i in range(2):
-            n2 = self.gots[i].shape[1]
-            self.send(i, self.shards[i].at[:, off(self.t.o, n2)], self.gots[i], self.t.sib)
+        dp, do, du, dd = self.far
+        for i, ref in enumerate((dp, do, du)):
+            self.send(i, ref, self.gots[i], self.t.sib)
+        self.send(3, dd.at[:, off(self.t.o, 384)], self.gots[3], self.t.sib)
 
     def join(self):
         t = self.t
-        for i in range(2):
+        dp, do, du, dd = self.shards
+        for i in range(4):
             self.arrived(i, self.gots[i])
-            join_pair(t, self.shards[i], self.gots[i], self.tmps[i], self.stages[i].at[t.z])
-
-    def spread(self, i):
-        own = self.stages[i].at[self.t.z]
-        for dev in self.t.zn:
-            self.send(2 + i, own, own, dev)
-
-    def plane(self):
+        main, down = self.stages
+        tmp = self.tmps[0]
+        mine, other = off(t.c, 24, 8), off(t.o, 24, 8)
+
+        def place(ref, got, a, n, b):
+            tmp[mine, 0:n] = ref[:, a : a + n].astype(F32)
+            tmp[other, 0:n] = got[:, a : a + n].astype(F32)
+            wide = -(-n // 128) * 128
+            main[t.z, :, b : b + wide] = tmp[:, 0:wide].astype(BF)
+
+        @pl.when(t.c == 0)
+        def _():
+            tmp[...] = jnp.zeros(tmp.shape, F32)
+            for r in range(4):
+                for g in range(3):
+                    place(dp, self.gots[0], 768 * g + 192 * r, 192, 768 * r + 256 * g)
+            place(do, self.gots[1], 0, 384, 3072)
+
+        @pl.when(t.c == 1)
+        def _():
+            for r in range(4):
+                place(du, self.gots[2], 768 * r, 768, 768 * r)
+            place(do, self.gots[1], 384, 384, 3072)
+
+        join_pair(t, dd, self.gots[3], self.tmps[1], down.at[t.z])
+
+    def spread(self, k):
+        self.z_spread((4 + k), self.views[k])
+
+    def relay(self, k):
+        self.z_relay(4 + k, 11 + k, self.views[k])
+
+    def plane(self, w):
         t = self.t
         main, down = self.stages
-        for i in range(2):
-            self.arrived(2 + i, self.stages[i].at[pl.ds(0, 3)])
-        self.local = []
+        self.z_last(4 + w, 11 + w, self.views[w])
+        if w == 0:
+            self.local = []
         for k in (1, 2, 3, 0):
+            if w < 4 and k != (1, 2, 3, 0)[w]:
+                continue
             q = t.qq[k]
-            moves = (
-                (main.at[:, :, off(q, 768)], self.dpu.at[t.c, :, t.q]),
-                (main.at[q, :, pl.ds(3072, 384)], self.do.at[t.c, pl.ds(pl.multiple_of(48 * t.q, 16), 48)]),
-                (down.at[q], self.dd.at[t.c, t.q]),
-            )
-            for i, (src, dst) in enumerate(moves):
-                if k:
-                    self.send(4 + i, src, dst, t.plane[k])
-                else:
-                    d = pltpu.make_async_copy(src, dst, self.ls.at[i])
-                    d.start()
-                    self.local.append(d)
+            if w < 4:
+                src, dst, at = main.at[:, :, off(q, 768)], self.dpu.at[t.c, :, t.q], 18
+            elif w == 4:
+                src, at = main.at[q, :, pl.ds(3072, 384)], 19
+                dst = self.do.at[t.c, pl.ds(pl.multiple_of(48 * t.q, 16), 48)]
+            else:
+                rows = pl.ds(96 * (w - 5), 96)
+                src, dst, at = down.at[q, rows], self.dd.at[t.c, t.q, rows], 15 + w
+            if k:
+                self.send(at, src, dst, t.plane[k])
+            else:
+                d = pltpu.make_async_copy(src, dst, self.ls.at[at - 18])
+                d.start()
+                self.local.append(d)
 
     def share(self):
         t = self.t
-        self.arrived(4, self.dpu.at[t.c, :, pl.ds(0, 3)])
-        self.arrived(5, self.do.at[t.c, pl.ds(0, 144)])
-        self.arrived(6, self.dd.at[t.c, pl.ds(0, 3)])
+        self.arrived(18, self.dpu.at[t.c, :, pl.ds(0, 3)])
+        self.arrived(19, self.do.at[t.c, pl.ds(0, 144)])
+        for j in range(2):
+            self.arrived(20 + j, self.dd.at[t.c, pl.ds(0, 3), pl.ds(0, 96)])
         for d in self.local:
             d.wait()
         for i, ref in enumerate((self.dpu, self.do, self.dd)):
             view = ref.at[t.c, pl.ds(0, 192)] if i == 1 else ref.at[t.c]
-            self.send(7 + i, view, view, t.sib)
-
-    def finish(self):
-        for i, ref in enumerate((self.dpu, self.do, self.dd)):
-            view = ref.at[self.t.o, pl.ds(0, 192)] if i == 1 else ref.at[self.t.o]
-            self.arrived(7 + i, view)
+            self.send(22 + i, view, view, t.sib)
+
+    def finish(self, i):
+        ref = (self.dpu, self.do, self.dd)[i]
+        view = ref.at[self.t.o, pl.ds(0, 192)] if i == 1 else ref.at[self.t.o]
+        self.arrived(22 + i, view)
 
 
 class Reduce(Sender):
-    def __init__(self, t, w, rc_, r1, r2, r3, fin, fin2, out, ss, rs):
+    def __init__(self, t, w, rc_, r1, r2, r3, fin, fin2, out, windows, ss, rs):
         super().__init__(t, ss, rs)
         self.w, self.rc, self.r1, self.r2, self.r3 = w, rc_, r1, r2, r3
-        self.fin, self.fin2, self.out = fin, fin2, out
-
-    def pair(self):
-        self.send(0, self.w.at[self.t.o], self.rc, self.t.sib)
-
-    def add(self, q, part):
+        self.fin, self.fin2, self.out, self.windows = fin, fin2, out, windows
+        self.by_rows = fin2.shape[0] == 96
+
+    def cut(self, ref, k, *lead):
+        rows, cols = self.windows[k]
+        lead += (slice(None),) * (len(ref.shape) - 2 - len(lead))
+        return ref.at[lead + (pl.ds(*rows), pl.ds(*cols))]
+
+    def pair(self, k):
+        self.send((k, 0), self.cut(self.w, k, self.t.o), self.cut(self.rc, k), self.t.sib)
+
+    def pair_rows(self, z):
+        self.send((z, 0), self.w.at[self.t.o, z], self.rc.at[z], self.t.sib)
+
+    def add(self, k, q, part):
+        (r, rn), (a, an) = self.windows[k]
         w, c = self.w, self.t.c
 
         @pl.loop(0, 4)
         def _(z):
-            w[c, z, q] = (w[c, z, q].astype(F32) + part[z].astype(F32)).astype(w.dtype)
-
-    def first(self):
+            at = (c, z, q, pl.ds(r, rn), pl.ds(a, an))
+            w[at] = (w[at].astype(F32) + part[z, r : r + rn, a : a + an].astype(F32)).astype(w.dtype)
+
+    def first(self, k):
         t = self.t
-        self.arrived(0, self.rc)
+        if self.by_rows:
+            for z in range(4 if k == 0 else 0):
+                self.arrived((z, 0), self.rc.at[z])
+        else:
+            self.arrived((k, 0), self.cut(self.rc, k))
         for i, q in ((0, t.q2), (1, t.q12)):
-            self.add(q, self.rc.at[:, q])
-            self.send(1 + i, self.w.at[t.c, :, q], self.r1.at[i], t.n2)
+            self.add(k, q, self.rc.at[:, q])
+            self.send(
+                (k, 1 + i), self.cut(self.w, k, t.c, slice(None), q), self.cut(self.r1, k, i, slice(None)), t.n2
+            )
         for q in (t.q, t.q1):
-            self.add(q, self.rc.at[:, q])
-
-    def second(self):
+            self.add(k, q, self.rc.at[:, q])
+
+    def second(self, k):
         t = self.t
-        self.arrived(2, self.r1.at[1])
-        self.add(t.q1, self.r1.at[1])
-        self.send(3, self.w.at[t.c, :, t.q1], self.r2, t.n1)
-        self.arrived(1, self.r1.at[0])
-        self.add(t.q, self.r1.at[0])
-
-    def third(self):
+        self.arrived((k, 2), self.cut(self.r1, k, 1, slice(None)))
+        self.add(k, t.q1, self.r1.at[1])
+        self.send((k, 3), self.cut(self.w, k, t.c, slice(None), t.q1), self.cut(self.r2, k, slice(None)), t.n1)
+        self.arrived((k, 1), self.cut(self.r1, k, 0, slice(None)))
+        self.add(k, t.q, self.r1.at[0])
+
+    def third(self, k):
         t = self.t
-        self.arrived(3, self.r2)
-        self.add(t.q, self.r2)
-        for k in range(3):
-            self.send(4, self.w.at[t.c, t.zz[k], t.q], self.r3.at[2 - k], t.zn[k])
-
-    def fourth(self):
+        self.arrived((k, 3), self.cut(self.r2, k, slice(None)))
+        self.add(k, t.q, self.r2)
+        for i in range(3):
+            self.send((k, 4), self.cut(self.w, k, t.c, t.zz[i], t.q), self.cut(self.r3, k, 2 - i), t.zn[i])
+
+    def fourth(self, k):
         t = self.t
-        self.arrived(4, self.r3)
-        total = self.w[t.c, t.z, t.q].astype(F32)
-        for k in range(3):
-            total = total + self.r3[k].astype(F32)
-        self.fin[...] = total
-        rd = self.fin.shape[0] // 2
-        self.send(5, self.fin.at[off(t.o, rd, 8)], self.fin2, t.sib)
+        (r, rn), (a, an) = self.windows[k]
+        self.arrived((k, 4), self.cut(self.r3, k, slice(None)))
+        total = self.w[t.c, t.z, t.q, r : r + rn, a : a + an].astype(F32)
+        for i in range(3):
+            total = total + self.r3[i, r : r + rn, a : a + an].astype(F32)
+        self.fin[r : r + rn, a : a + an] = total
+        if k == len(self.windows) - 1:
+            rd = self.fin.shape[0] // 2
+            self.send((0, 5), self.fin.at[off(t.o, rd, 8)], self.fin2, t.sib)
 
     def fifth(self):
         t = self.t
         rd, n2 = self.fin2.shape
-        self.arrived(5, self.fin2)
+        self.arrived((0, 5), self.fin2)
         self.out[:, off(t.c, n2)] = self.fin[off(t.c, rd, 8), :]
         self.out[:, off(t.o, n2)] = self.fin2[...]
 
@@ -304,7 +428,8 @@
     [((48 * j, 48), (0, 384)) for j in range(4)],
 )
 SCRATCH = {
-    "got": [((rd, n2), dt) for rd, n2, dt in SIZES] + [((24, 3456), BF), ((96, 384), BF)],
+    "got": [((rd, n2), dt) for rd, n2, dt in SIZES]
+    + [((24, 2304), BF), ((24, 768), BF), ((24, 3072), BF), ((96, 384), BF)],
     "w": [((2, 4, 4, 2 * rd, n2), dt) for rd, n2, dt in SIZES],
     "fin": [((2 * rd, n2), F32) for rd, n2, dt in SIZES],
     "fin2": [((rd, n2), F32) for rd, n2, dt in SIZES],
@@ -338,28 +463,33 @@
     "pairs": [((2, 2, 768), F32)] * 2,
     "soo": [((2, 768), F32)],
     "mat": [((32, 768), F32)] * 2,
-    "ars": [((4, 32, 768), BF)],
-    "arb": [((4, 3, 32, 768), BF)],
+    "ars": [((3, 32, 768), BF)],
+    "gpc": [((64, 3072), BF)],
+    "lowc": [((64, 768), BF)],
+    "arb": [((3, 3, 32, 768), BF)],
     "fq": [((2, 4, 4, 32, 1280), BF)],
     "fz": [((2, 4, 32, 1536), BF)],
     "vg": [((128, 768), F32)],
     "flip": [((768, 128), F32)],
 }
 SEMS = {
-    "gs": (5, 4, 9),
-    "gr": (5, 4, 9),
-    "ds": (10,),
-    "dr": (10,),
+    "gs": (5, 4, 10),
+    "gr": (5, 4, 10),
+    "ds": (25,),
+    "dr": (25,),
     "ls": (4,),
-    "rs": (5, 6),
-    "rr": (5, 6),
+    "rs": (5, 4, 6),
+    "rr": (5, 4, 6),
     "xs": (12,),
     "xr": (12,),
-    "fs": (2, 9),
-    "fr": (2, 9),
-    "os": (8,),
+    "fs": (3, 10),
+    "fr": (3, 10),
+    "es": (3, 3),
+    "er": (3, 3),
+    "os": (11,),
+    "ins": (13,),
 }
-INS = ("tok", "cot", "tmask", "dmask", "small", "sp", "so", "su", "sd", "dmain", "ddown")
+INS = ("tok", "cot", "tmask", "dmask", "small", "sp", "so", "su", "sd", "dp", "dout", "du", "ddown")
 OUTS = (
     ("out", (512, 768), BF),
     ("gin", (512, 768), F32),
@@ -368,7 +498,7 @@
     ("gso", (24, 768), F32),
     ("gsu", (24, 3072), F32),
     ("gsd", (96, 768), F32),
-    ("gdp", (24, 3072), F32),
+    ("gdp", (24, 2304), F32),
     ("gdo", (24, 768), F32),
     ("gdu", (24, 3072), F32),
     ("gdd", (96, 768), F32),
@@ -376,7 +506,15 @@
 
 
 class Box:
-    pass
+    def put(self, name, ref):
+        at = [out[0] for out in OUTS].index(name)
+        d = pltpu.make_async_copy(ref, self.back[name], self.os.at[at])
+        d.start()
+        self.flying[name] = d
+
+    def ready(self, *names):
+        for name in names:
+            self.coming[name].wait()
 
 
 def kernel(*refs):
@@ -387,149 +525,236 @@
         got, refs[:n] = refs[:n], []
         return got
 
+    b.far = {name: take(1)[0] for name in INS}
+    b.back = {name: take(1)[0] for name, _, _ in OUTS}
     for name in INS:
         setattr(b, name, take(1)[0])
-    for name, _, _ in OUTS:
+    for name, _, _ in OUTS[2:]:
         setattr(b, name, take(1)[0])
     for name, items in SCRATCH.items():
         got = take(len(items))
         setattr(b, name, got if len(got) > 1 else got[0])
     for name in SEMS:
         setattr(b, name, take(1)[0])
-    b.credit = take(1)[0]
+    b.credit, b.met, b.met2 = take(3)
     b.t = Spot()
     run(b)
+
+
+FACTOR_WINDOWS = [((0, 32), (0, 512)), ((0, 32), (512, 384)), ((0, 32), (896, 384))]
+LINE_WINDOWS = [(0, 768), (768, 384), (1152, 384)]
 
 
 def run(b):
     t = b.t
     b.x = Sender(t, b.xs, b.xr)
+    b.flying, b.coming = {}, {}
+    for i, name in enumerate(INS):
+        d = pltpu.make_async_copy(b.far[name], getattr(b, name), b.ins.at[i])
+        d.start()
+        b.coming[name] = d
     b.do[...] = jnp.zeros(b.do.shape, BF)
     b.vg[...] = jnp.zeros(b.vg.shape, F32)
     enter(t)
+    pass_on(t, b.met)
     shards = (b.small, b.sp, b.so, b.su, b.sd)
+    far = [b.far[name] for name in ("small", "sp", "so", "su", "sd")]
     gs = [
-        Gather(t, shards[i], b.w[i], b.got[i], b.fin[i], WINDOWS[i], b.gs.at[i], b.gr.at[i])
+        Gather(t, far[i], shards[i], b.w[i], b.got[i], b.fin[i], WINDOWS[i], b.gs.at[i], b.gr.at[i])
         for i in range(5)
     ]
     dg = DocGather(
-        t, (b.dmain, b.ddown), b.stage, b.got[5:], (b.fin[1], b.fin[4]), b.dpu, b.do, b.dd, b.ds, b.dr, b.ls
-    )
-    for g in gs[:2]:
-        g.pair()
-    for g in gs[2:]:
+        t,
+        [b.far[name] for name in ("dp", "dout", "du", "ddown")],
+        (b.dp, b.dout, b.du, b.ddown),
+        b.stage,
+        b.got[5:],
+        (b.fin[1], b.fin[4]),
+        b.dpu,
+        b.do,
+        b.dd,
+        b.ds,
+        b.dr,
+        b.ls,
+    )
+    for g in gs:
         g.pair()
     dg.pair()
+    b.f = Gather(t, None, None, b.fq, None, None, FACTOR_WINDOWS, b.fs, b.fr)
+    b.e = LineGather(t, b.fz, LINE_WINDOWS, b.es, b.er)
+
     events = [(g, k) for g in gs for k in range(len(g.windows))]
-    clock = [0]
-
-    def do(name, at):
-        if 0 <= at < len(events):
-            getattr(events[at][0], name)(events[at][1])
+    lines = events + [(dg, k) for k in range(7)]
+    clock, spreads, relays = [0], [0], [0]
+
+    def do(name, at, among=events):
+        if 0 <= at < len(among):
+            getattr(among[at][0], name)(among[at][1])
+
+    def relay(n):
+        for _ in range(n):
+            do("relay", relays[0], lines)
+            relays[0] += 1
+            do("spread", spreads[0], lines)
+            spreads[0] += 1
 
     def tick(upto):
         while clock[0] <= upto:
             at = clock[0]
+            busy = relays[0] < len(events)
             do("first", at)
-            do("spread", at + 2)
-            if at + 2 == len(events):
-                dg.spread(0)
-                dg.spread(1)
-            do("second", at - 1)
-            do("third", at - 2)
-            do("finish", at - 3)
+            relay(1)
+            do("second", at - 2)
+            if busy:
+                relay(1)
+            do("third", at - 4)
+            do("finish", at - 5)
             clock[0] += 1
 
+    b.ready("small", "sp")
     gs[0].join()
     gs[1].join()
-    do("spread", 0)
-    do("spread", 1)
+    for i in range(3):
+        do("spread", i, lines)
+    spreads[0] = 3
+    b.ready("so", "su", "sd")
     for g in gs[2:]:
         g.join()
+    pl.semaphore_wait(b.met, 4)
+    pass_on(t, b.met2)
+    relay(1)
+    tick(0)
+    b.ready("dp", "dout", "du", "ddown")
     dg.join()
+    tick(1)
+    pl.semaphore_wait(b.met2, 4)
+    b.ready("cot", "tok", "tmask", "dmask")
     send_cotangents(b)
-    tick(3)
+    tick(5)
     vectors_in(b)
-    tick(6)
+    tick(8)
     segment_project(b)
+    tick(9)
     for seg in range(4):
         attend(b, seg)
-        tick(7 + seg // 2)
+        tick(10 + seg // 2)
     segment_mix(b)
-    tick(9)
     for j in range(4):
         segment_up(b, j)
-        tick(10 + j)
-    tick(14)
-    dg.plane()
-    tick(15)
-    segment_down(b)
-    send_summaries(b)
+        tick(12 + j)
+        if j:
+            dg.plane(j - 1)
+    dg.plane(3)
+    tick(16)
+    for k in range(4, 7):
+        dg.plane(k)
+    tick(17)
+    send_summaries(b, summary_rows(b))
+    steps = document(b)
+    segment_down(b, 0)
     dg.share()
     for g in gs:
         g.drain()
-    dg.finish()
+    for i in range(3):
+        dg.finish(i)
     dg.drain()
-    document(b)
+    next(steps)
+    segment_down(b, 1)
+    next(steps)
+    second_back(b)
+    next(steps)
+    hidden_back(b)
+    next(steps)
+    first_back(b)
+    next(steps)
+    next(steps, None)
     finish_output(b)
+    b.f.spread(2)
+    b.e.spread(2)
 
     small_rc, up_rc, down_rc = b.rc
     rcs = (small_rc, up_rc.at[:, :, :, 0:1152], up_rc.at[:, :, :, 1152:1536], up_rc, down_rc)
     rs = [
-        Reduce(t, b.w[i], rcs[i], b.r1[i], b.r2[i], b.r3[i], b.fin[i], b.fin2[i], out, b.rs.at[i], b.rr.at[i])
+        Reduce(
+            t,
+            b.w[i],
+            rcs[i],
+            b.r1[i],
+            b.r2[i],
+            b.r3[i],
+            b.fin[i],
+            b.fin2[i],
+            out,
+            WINDOWS[i],
+            b.rs.at[i],
+            b.rr.at[i],
+        )
         for i, out in enumerate((b.gsmall, b.gsp, b.gso, b.gsu, b.gsd))
     ]
+    for r, name in zip(rs, ("gsmall", "gsp", "gso", "gsu", "gsd")):
+        r.name = name
     rsmall, rproject, routput, rup, rdown = rs
-    second_back(b)
-    hidden_back(b)
-    down_terms(b)
-    rdown.pair()
-    first_back(b)
-    rdown.first()
-    up_terms(b)
-    rup.pair()
+    terms = [(r, k) for r in (rdown, rup, routput, rproject, rsmall) for k in range(len(r.windows))]
+    clock[0] = 0
+
+    ends = {id(r): max(i for i, e in enumerate(terms) if e[0] is r) for r in rs}
+
+    def tock(upto):
+        while clock[0] <= upto:
+            at = clock[0]
+            do("first", at, terms)
+            do("second", at - 2, terms)
+            do("third", at - 4, terms)
+            do("fourth", at - 6, terms)
+            for r in rs:
+                if ends[id(r)] == at - 7:
+                    r.fifth()
+                    b.put(r.name, r.out)
+            clock[0] += 1
+
+    second_back_rows(b)
+    hidden_back_rows(b)
+    b.f.relay(2)
+    b.e.relay(2)
+    b.f.second(1)
+    b.f.third(0)
+    down_terms(b, rdown)
+    first_back_rows(b)
+    b.f.first(2)
+    b.e.first(2)
+    b.f.third(1)
+    tock(0)
+    column_terms(b, rup, b.fl, b.gp)
+    tock(1)
+    b.f.second(2)
     mixed_back(b)
-    rdown.second()
-    output_terms(b)
-    rup.first()
+    tock(2)
+    context_back(b)
+    tock(3)
+    b.f.third(2)
+    attend_back(b, 0)
+    tock(4)
+    attend_back(b, 1)
+    tock(5)
+    attend_back(b, 2)
+    tock(6)
+    attend_back(b, 3)
+    tock(7)
     pl.semaphore_signal(b.credit, inc=1, device_id=t.sib, device_id_type=MESH)
     pl.semaphore_wait(b.credit, 1)
-    routput.pair()
-    rdown.third()
-    attend_back(b, 0)
-    attend_back(b, 1)
-    rup.second()
-    routput.first()
-    rdown.fourth()
-    attend_back(b, 2)
-    attend_back(b, 3)
-    project_terms(b)
-    rproject.pair()
-    rup.third()
-    routput.second()
-    rdown.fifth()
+    column_terms(b, routput, b.ctx, b.low)
+    input_back(b)
+    column_terms(b, rproject, b.tok, b.pr)
+    tock(8)
     vectors_out(b)
-    rsmall.pair()
-    rproject.first()
-    routput.third()
-    rup.fourth()
+    rsmall.pair(0)
+    tock(10)
     document_terms(b)
-    rsmall.first()
-    rproject.second()
-    routput.fourth()
-    rup.fifth()
-    rsmall.second()
-    rproject.third()
-    routput.fifth()
-    rsmall.third()
-    rproject.fourth()
-    rsmall.fourth()
-    rproject.fifth()
-    rsmall.fifth()
+    tock(len(terms) + 6)
     for r in rs:
         r.drain()
     b.x.drain()
-    for d in b.flying:
+    for d in b.flying.values():
         d.wait()
 
 
@@ -644,43 +869,55 @@
             b.gp[rows, cols] = slope.astype(BF)
 
 
-def segment_down(b):
+def summary_rows(b):
     w = b.w[4]
-
-    @pl.loop(0, 4)
-    def _(i):
-        h, r = lax.div(i, 2), lax.rem(i, 2)
-        rows = off(r, 256, 256)
+    for s in range(4):
+        b.gpc[16 * s : 16 * s + 16, :] = b.act[128 * s : 128 * s + 16, :]
+    parts = [dot(b.gpc[...], w[h].reshape(3072, 384)) for h in range(2)]
+    both = jnp.concatenate(parts, axis=1)
+    for s in range(4):
+        b.gpc[16 * s : 16 * s + 16, :] = b.gp[128 * s : 128 * s + 16, :]
+    rows = []
+    for s in range(4):
+        n, _ = normed(b.row[128 * s : 128 * s + 8, :] + both[16 * s : 16 * s + 8])
+        rows.append((n * vec(b, 2) + vec(b, 3))[0:1])
+    return rows
+
+
+def segment_down(b, r):
+    w = b.w[4]
+    rows = pl.ds(256 * r, 256)
+
+    @pl.loop(0, 2)
+    def _(h):
         b.row[rows, off(h, 384)] += dot(b.act[rows, :], w[h].reshape(3072, 384))
 
     gain, shift = vec(b, 2), vec(b, 3)
 
-    @pl.loop(0, 16)
+    @pl.loop(8 * r, 8 * r + 8)
     def _(i):
         rows = off(i, 32, 32)
         n, inverse = normed(b.row[rows, :])
         b.n2[rows, :] = n.astype(BF)
         b.i2[rows, :] = inverse
-        second = n * gain + shift
-        b.row[rows, :] = second
-        b.ob[rows, :] = second.astype(BF)
-
-
-def send_summaries(b):
-    t = b.t
-    places = b.table[t.i]
+        b.ob[rows, :] = (n * gain + shift).astype(BF)
+
+
+def send_summaries(b, rows):
+    places = b.table[b.t.i]
     for m in range(2):
         for s in range(2):
-            rows = b.row[pl.ds(128 * (2 * m + s), 8), :]
-            b.src[1][m, s : s + 1, :] = rows[0:1] + places[s : s + 1]
+            b.src[1][m, s : s + 1, :] = rows[2 * m + s] + places[s : s + 1]
     send_rows(b, 1)
 
 
-def plane_sum(b, n, partial):
-    t = b.t
+def plane_send(b, n, partial):
     b.ars[n] = partial.astype(BF)
     for k in (1, 2, 3):
-        b.x.send(2 + n, b.ars.at[n], b.arb.at[n, k - 1], t.plane[k])
+        b.x.send(2 + n, b.ars.at[n], b.arb.at[n, k - 1], b.t.plane[k])
+
+
+def plane_take(b, n):
     b.x.arrived(2 + n, b.arb.at[n])
     total = b.ars[n].astype(F32)
     for k in range(3):
@@ -707,29 +944,60 @@
     three = dot(shares_low, v3)
     ctx = sum(three[32 * h : 32 * h + 32] * heads[h].astype(F32) for h in range(3)).astype(BF)
     mixed = jnp.concatenate([dot(ctx, b.do[h]) for h in range(2)], axis=1)
-    n1, i1 = normed(h_in + plane_sum(b, 0, mixed))
+    plane_send(b, 0, mixed)
+    yield
+    n1, i1 = normed(h_in + plane_take(b, 0))
     first = n1 * vec(b, 4) + vec(b, 5)
     first_low = first.astype(BF)
     active, slope = gelu_pair(dot(first_low, du))
     active = active.astype(BF)
     branch = jnp.concatenate([dot(active, b.dd[h].reshape(768, 384)) for h in range(2)], axis=1)
-    n2, i2 = normed(first + plane_sum(b, 1, branch))
+    plane_send(b, 1, branch)
+
+    @pl.when(t.c == 0)
+    def _():
+        b.fq[0, t.z, t.q, :, 0:512] = active[:, 0:512]
+        b.fz[0, t.z, :, 0:768] = h_low
+
+    @pl.when(t.c == 1)
+    def _():
+        b.fq[1, t.z, t.q, :, 0:256] = active[:, 512:768]
+        b.fq[1, t.z, t.q, :, 256:512] = ctx
+        b.fz[1, t.z, :, 0:768] = first_low
+
+    b.f.spread(0)
+    b.e.spread(0)
+    yield
+    n2, i2 = normed(first + plane_take(b, 1))
     out = n2 * vec(b, 6) + vec(b, 7)
+    g = take_rows(b, 0)
+    delta = norm_back(g, n2, i2, vec(b, 6))
+    branch_low = delta.astype(BF)
+    back = sum(dot_rt(branch_low[:, 384 * h : 384 * h + 384], b.dd[h].reshape(768, 384)) for h in range(2))
+    hidden_delta = (back * slope).astype(BF)
+    plane_send(b, 2, dot_rt(hidden_delta, du))
+    b.vg[6:7, :] = jnp.sum(g * n2, axis=0, keepdims=True) * 0.125
+    b.vg[7:8, :] = jnp.sum(g, axis=0, keepdims=True) * 0.125
     for i in range(16):
         b.slots[2][i] = out[2 * i : 2 * i + 2]
     other_i = 8 * (1 - t.half) + 2 * t.q + t.c
     b.x.send(6, b.slots[2].at[other_i], b.soo, (4 * t.zo + t.q, t.c))
 
-    g = take_rows(b, 0)
-    b.vg[6:7, :] = jnp.sum(g * n2, axis=0, keepdims=True) * 0.125
-    b.vg[7:8, :] = jnp.sum(g, axis=0, keepdims=True) * 0.125
-    delta = norm_back(g, n2, i2, vec(b, 6))
-    branch_low = delta.astype(BF)
-    back = sum(dot_rt(branch_low[:, 384 * h : 384 * h + 384], b.dd[h].reshape(768, 384)) for h in range(2))
-    hidden_delta = (back * slope).astype(BF)
-    first_delta = delta + plane_sum(b, 2, dot_rt(hidden_delta, du))
-    b.vg[4:5, :] = jnp.sum(first_delta * n1, axis=0, keepdims=True) * 0.125
-    b.vg[5:6, :] = jnp.sum(first_delta, axis=0, keepdims=True) * 0.125
+    def halves(ref, at, value):
+        for h in range(2):
+
+            @pl.when(t.c == h)
+            def _():
+                ref[(h,) + at] = value[:, 384 * h : 384 * h + 384]
+
+    halves(b.fq, (t.z, t.q, slice(None), slice(512, 896)), hidden_delta)
+    halves(b.fz, (t.z, slice(None), slice(768, 1152)), branch_low)
+    b.f.relay(0)
+    b.e.relay(0)
+    b.f.spread(1)
+    b.e.spread(1)
+    yield
+    first_delta = delta + plane_take(b, 2)
     mixed_delta = norm_back(first_delta, n1, i1, vec(b, 4))
     mixed_low = mixed_delta.astype(BF)
     ctx_delta = sum(dot_rt(mixed_low[:, 384 * h : 384 * h + 384], b.do[h]) for h in range(2)).astype(BF)
@@ -752,37 +1020,26 @@
             8, b.slots[3].at[8 * (1 - t.half) + 2 * t.qq[k] + t.c], b.sdr.at[1, k], (4 * t.zo + t.qq[k], t.c)
         )
     b.sdr[0, 0] = b.slots[3][t.i]
-
-    @pl.when(t.c == 0)
-    def _():
-        b.fq[0, t.z, t.q, :, 0:768] = pd
-        b.fq[0, t.z, t.q, :, 768:1024] = ctx
-        b.fq[0, t.z, t.q, :, 1024:1280] = active[:, 0:256]
-        b.fz[0, t.z, :, 0:768] = h_low
-        b.fz[0, t.z, :, 768:1536] = mixed_low
-
-    @pl.when(t.c == 1)
-    def _():
-        b.fq[1, t.z, t.q, :, 0:768] = hidden_delta
-        b.fq[1, t.z, t.q, :, 768:1280] = active[:, 256:768]
-        b.fz[1, t.z, :, 0:768] = first_low
-        b.fz[1, t.z, :, 768:1536] = branch_low
-
-    b.f = Gather(t, None, b.fq, None, None, [((0, 32), (0, 1280))], b.fs, b.fr)
-    b.f.spread(0)
-    for dev in t.zn:
-        b.f.send((1, 0), b.fz.at[t.c, t.z], b.fz.at[t.c, t.z], dev)
+    b.vg[4:5, :] = jnp.sum(first_delta * n1, axis=0, keepdims=True) * 0.125
+    b.vg[5:6, :] = jnp.sum(first_delta, axis=0, keepdims=True) * 0.125
+    halves(b.fq, (t.z, t.q, slice(None), slice(896, 1280)), pd)
+    halves(b.fz, (t.z, slice(None), slice(1152, 1536)), mixed_low)
+    b.f.relay(1)
+    b.e.relay(1)
+    b.f.first(0)
+    b.e.first(0)
+    yield
+    b.f.second(0)
     b.x.arrived(6, b.soo)
     b.pairs[0][t.half] = b.slots[2][t.i]
     b.pairs[0][1 - t.half] = b.soo[...]
+    yield
     b.x.arrived(7, b.sdr.at[0, pl.ds(0, 3)])
     b.x.arrived(8, b.sdr.at[1])
     b.pairs[1][t.half] = b.sdr[0, 0] + b.sdr[0, 1] + b.sdr[0, 2] + b.sdr[0, 3]
     b.pairs[1][1 - t.half] = b.sdr[1, 0] + b.sdr[1, 1] + b.sdr[1, 2] + b.sdr[1, 3]
-    b.f.first(0)
-    b.f.arrived((1, 0), b.fz.at[t.c, pl.ds(0, 3)])
-    b.f.send((1, 1), b.fz.at[t.c], b.fz.at[t.c], t.sib)
-    b.f.second(0)
+    b.f.first(1)
+    b.e.first(1)
 
 
 def finish_output(b):
@@ -792,9 +1049,7 @@
             rows = pl.ds(128 * (2 * m + s), 16)
             fresh = jnp.where(first_row, b.pairs[0][m, s : s + 1, :], b.ob[rows, :].astype(F32))
             b.ob[rows, :] = fresh.astype(BF)
-    d = pltpu.make_async_copy(b.ob, b.out, b.os.at[0])
-    d.start()
-    b.flying = [d]
+    b.put("out", b.ob)
 
 
 def second_back(b):
@@ -803,11 +1058,8 @@
     def body(i, carry):
         gains, shifts = carry
         rows = off(i, 16, 16)
-        seg = lax.div(i, 8)
-        fresh = (lax.broadcasted_iota(jnp.int32, (16, 768), 0) + 16 * lax.rem(i, 8)) == 0
-        own = b.pairs[1][lax.div(seg, 2)]
-        own = jnp.where(lax.rem(seg, 2) == 0, own[0:1], own[1:2])
-        g = jnp.where(fresh, own, b.cot[rows, :].astype(F32))
+        late = (lax.broadcasted_iota(jnp.int32, (16, 768), 0) + 16 * lax.rem(i, 8)) == 0
+        g = jnp.where(late, 0.0, b.cot[rows, :].astype(F32))
         n = b.n2[rows, :].astype(F32)
         delta = norm_back(g, n, b.i2[rows, :], gain)
         b.row[rows, :] = delta
@@ -818,6 +1070,51 @@
     gains, shifts = lax.fori_loop(0, 32, body, (zero, zero))
     b.vg[2:3, :] = jnp.sum(gains, axis=0, keepdims=True)
     b.vg[3:4, :] = jnp.sum(shifts, axis=0, keepdims=True)
+
+
+def second_back_rows(b):
+    gain = vec(b, 2)
+    top = lax.broadcasted_iota(jnp.int32, (16, 768), 0) == 0
+    gains, shifts = b.vg[2:3, :], b.vg[3:4, :]
+    for s in range(4):
+        rows = slice(128 * s, 128 * s + 16)
+        g = b.pairs[1][s // 2, s % 2 : s % 2 + 1, :]
+        n = b.n2[rows, :].astype(F32)
+        delta = norm_back(jnp.where(top, g, 0.0), n, b.i2[rows, :], gain)
+        b.row[rows, :] = jnp.where(top, delta, b.row[rows, :])
+        low = jnp.where(top, delta, b.low[rows, :].astype(F32)).astype(BF)
+        b.low[rows, :] = low
+        b.lowc[16 * s : 16 * s + 16, :] = low
+        gains += g * n[0:1]
+        shifts += g
+    b.vg[2:3, :] = gains
+    b.vg[3:4, :] = shifts
+
+
+def hidden_back_rows(b):
+    w = b.w[4]
+
+    @pl.loop(0, 4)
+    def _(z):
+        cols = off(z, 768)
+        back = dot_rt(b.lowc[:, 0:384], w[0, z].reshape(768, 384)) + dot_rt(
+            b.lowc[:, 384:768], w[1, z].reshape(768, 384)
+        )
+        delta = (back * b.gpc[:, cols].astype(F32)).astype(BF)
+        b.gpc[:, cols] = delta
+        for s in range(4):
+            b.gp[pl.ds(128 * s, 16), cols] = delta[16 * s : 16 * s + 16]
+
+
+def first_back_rows(b):
+    w = b.w[3]
+    top = lax.broadcasted_iota(jnp.int32, (16, 768), 0) == 0
+    more = dot_rt(b.gpc[:, 0:1536], w[0].reshape(768, 1536)) + dot_rt(
+        b.gpc[:, 1536:3072], w[1].reshape(768, 1536)
+    )
+    for s in range(4):
+        rows = slice(128 * s, 128 * s + 16)
+        b.row[rows, :] += jnp.where(top, more[16 * s : 16 * s + 16], 0.0)
 
 
 def hidden_back(b):
@@ -834,14 +1131,14 @@
             b.gp[rows, cols] = (back * b.gp[rows, cols].astype(F32)).astype(BF)
 
 
-def down_terms(b):
-    w = b.w[4]
-
-    @pl.loop(0, 4)
-    def _(z):
-        a = b.act[:, off(z, 768)]
-        for h in range(2):
-            w[h, z] = dot_lt(a, b.low[:, 384 * h : 384 * h + 384]).astype(BF).reshape(4, 192, 384)
+def down_terms(b, r):
+    t, w = b.t, b.w[4]
+    for h in (t.o, t.c):
+        for z in range(4):
+            part = dot_lt(b.act[:, 768 * z : 768 * z + 768], b.low[:, off(h, 384)])
+            w[h, z] = part.astype(BF).reshape(4, 192, 384)
+            if h is t.o:
+                r.pair_rows(z)
 
 
 def first_back(b):
@@ -852,16 +1149,6 @@
         rows = off(r, 256, 256)
         for h in range(2):
             b.row[rows, :] += dot_rt(b.gp[rows, 1536 * h : 1536 * h + 1536], w[h].reshape(768, 1536))
-
-
-def up_terms(b):
-    w = b.w[3]
-
-    @pl.loop(0, 8)
-    def _(i):
-        h, j = lax.div(i, 4), lax.rem(i, 4)
-        part = dot_lt(b.fl[...], b.gp[:, off(i, 384)])
-        w[h, :, :, :, off(j, 384)] = part.astype(BF).reshape(4, 4, 48, 384)
 
 
 def mixed_back(b):
@@ -883,18 +1170,15 @@
     b.vg[1:2, :] = jnp.sum(offsets, axis=0, keepdims=True)
 
 
-def output_terms(b):
+def context_back(b):
     w = b.w[2]
-    b.flying[0].wait()
-    b.flying = []
+    b.flying.pop("out").wait()
     for r in range(2):
         rows = pl.ds(256 * r, 256)
         back = dot_rt(b.low[rows, 0:384], w[0].reshape(768, 384)) + dot_rt(
             b.low[rows, 384:768], w[1].reshape(768, 384)
         )
         b.ob[rows, :] = back.astype(BF)
-    for h in range(2):
-        w[h] = dot_lt(b.ctx[...], b.low[:, 384 * h : 384 * h + 384]).astype(BF).reshape(4, 4, 48, 384)
 
 
 def attend_back(b, seg):
@@ -921,7 +1205,7 @@
         b.pr[rows, off(p + 12, 128)] = dot_lt(shares_low, cs).astype(BF)
 
 
-def project_terms(b):
+def input_back(b):
     w = b.w[1]
 
     @pl.loop(0, 2)
@@ -930,15 +1214,18 @@
         for h in range(2):
             b.row[rows, :] += dot_rt(b.pr[rows, 1152 * h : 1152 * h + 1152], w[h].reshape(768, 1152))
 
-    d = pltpu.make_async_copy(b.row, b.gin, b.os.at[1])
-    d.start()
-    b.flying = [d]
-
-    @pl.loop(0, 6)
-    def _(i):
-        h, j = lax.div(i, 3), lax.rem(i, 3)
-        part = dot_lt(b.tok[...], b.pr[:, off(i, 384)])
-        w[h, :, :, :, off(j, 384)] = part.astype(BF).reshape(4, 4, 48, 384)
+    b.put("gin", b.row)
+
+
+def column_terms(b, r, left, right):
+    t, w = b.t, r.w
+    n = len(r.windows)
+    for h in (t.o, t.c):
+        for j in range(n):
+            part = dot_lt(left[...], right[:, off(n * h + j, 384)])
+            w[h, :, :, :, pl.ds(384 * j, 384)] = part.astype(BF).reshape(4, 4, 48, 384)
+            if h is t.o:
+                r.pair(j)
 
 
 def vectors_out(b):
@@ -953,42 +1240,57 @@
 
 def document_terms(b):
     t = b.t
-    b.f.third(0)
-    b.f.finish(0)
-    b.f.arrived((1, 1), b.fz.at[t.o])
+    for k in range(3):
+        b.f.finish(k)
+        b.e.finish(k)
     b.f.drain()
+    b.e.drain()
     own = 24 * t.dev
     part = 24 * lax.rem(t.dev, 8)
+    fq, fz = b.fq, b.fz
 
     def rows_of(value, at, size):
         n = value.shape[1]
         b.flip[0:n, :] = jnp.transpose(value.astype(F32))
         return b.flip[pl.ds(pl.multiple_of(at, 8), size), :].astype(BF)
 
-    left = rows_of(b.fz[0, :, :, 0:768].reshape(128, 768), own, 24)
+    def line(a):
+        both = [fz[h, :, :, a : a + 384].reshape(128, 384) for h in range(2)]
+        return jnp.concatenate(both, axis=1)
+
+    def rank(q, a):
+        both = [fq[h, :, q, :, a : a + 384].reshape(128, 384) for h in range(2)]
+        return jnp.concatenate(both, axis=1)
+
+    left = rows_of(fz[0, :, :, 0:768].reshape(128, 768), own, 24)
     for q in range(4):
-        b.gdp[:, 768 * q : 768 * q + 768] = dot(left, b.fq[0, :, q, :, 0:768].reshape(128, 768))
-    left = rows_of(b.fq[0, :, t.z, :, 768:1024].reshape(128, 256), part, 24)
-    b.gdo[...] = dot(left, b.fz[0, :, :, 768:1536].reshape(128, 768))
-    left = rows_of(b.fz[1, :, :, 0:768].reshape(128, 768), own, 24)
+        part_q = dot(left, rank(q, 896))
+        for g in range(3):
+            b.gdp[:, 768 * g + 192 * q : 768 * g + 192 * q + 192] = part_q[:, 256 * g : 256 * g + 192]
+    left = rows_of(fq[1, :, t.z, :, 256:512].reshape(128, 256), part, 24)
+    b.gdo[...] = dot(left, line(1152))
+    left = rows_of(fz[1, :, :, 0:768].reshape(128, 768), own, 24)
     for q in range(4):
-        b.gdu[:, 768 * q : 768 * q + 768] = dot(left, b.fq[1, :, q, :, 0:768].reshape(128, 768))
-    active = jnp.concatenate((b.fq[0, :, t.z, :, 1024:1280], b.fq[1, :, t.z, :, 768:1280]), axis=-1)
+        b.gdu[:, 768 * q : 768 * q + 768] = dot(left, rank(q, 512))
+    active = jnp.concatenate((fq[0, :, t.z, :, 0:512], fq[1, :, t.z, :, 0:256]), axis=-1)
     left = rows_of(active.reshape(128, 768), 4 * part, 96)
-    b.gdd[...] = dot(left, b.fz[1, :, :, 768:1536].reshape(128, 768))
+    b.gdd[...] = dot(left, line(768))
+    for name in ("gdp", "gdo", "gdu", "gdd"):
+        b.put(name, getattr(b, name))
 
 
 def mega(*arrays):
-    vm = pl.BlockSpec(memory_space=pltpu.VMEM)
     an = pl.BlockSpec(memory_space=pl.ANY)
     return pl.pallas_call(
         kernel,
         out_shape=[jax.ShapeDtypeStruct(shape, dt) for _, shape, dt in OUTS],
-        in_specs=[vm] * len(INS),
-        out_specs=[an, an] + [vm] * (len(OUTS) - 2),
-        scratch_shapes=[pltpu.VMEM(shape, dt) for items in SCRATCH.values() for shape, dt in items]
+        in_specs=[an] * len(INS),
+        out_specs=[an] * len(OUTS),
+        scratch_shapes=[pltpu.VMEM(item.shape, item.dtype) for item in arrays]
+        + [pltpu.VMEM(shape, dt) for _, shape, dt in OUTS[2:]]
+        + [pltpu.VMEM(shape, dt) for items in SCRATCH.values() for shape, dt in items]
         + [pltpu.SemaphoreType.DMA(shape) for shape in SEMS.values()]
-        + [pltpu.SemaphoreType.REGULAR],
+        + [pltpu.SemaphoreType.REGULAR] * 3,
         compiler_params=pltpu.CompilerParams(
             collective_id=1, has_side_effects=True, vmem_limit_bytes=65200 * 1024
         ),
@@ -1008,19 +1310,11 @@
     )
     dmask = (doc > 0).astype(F32)
     rows = weights[0].shape[0]
-    vectors = jnp.stack([weights[i] for i in (4, 5, 6, 7, 12, 13, 14, 15)], axis=1)
-    small = jnp.concatenate(
-        (
-            vectors,
-            jnp.zeros((rows, 120), BF),
-            weights[16],
-            jnp.zeros((rows, 96), BF),
-        ),
-        axis=1,
-    ).astype(F32)
-    project = jnp.pad(weights[8].reshape(rows, 3, 4, 192), ((0, 0), (0, 0), (0, 0), (0, 64)))
-    project = jnp.transpose(project, (0, 2, 1, 3)).reshape(rows, 3072)
-    dmain = jnp.concatenate((project, weights[9][:, :384], weights[10], weights[9][:, 384:]), axis=1)
+    lane = jnp.arange(256)[None]
+    small = jnp.pad(weights[16], ((0, 0), (128, 96)))
+    for at, i in enumerate((4, 5, 6, 7, 12, 13, 14, 15)):
+        small = jnp.where(lane == at, weights[i][:, None], small)
+    small = small.astype(F32)
     outs = mega(
         tokens.reshape(-1, width),
         cotangent.reshape(-1, width),
@@ -1028,12 +1322,9 @@
         dmask,
         small,
         *weights[:4],
-        dmain,
-        weights[11],
+        *weights[8:12],
     )
     out, gin, gsmall, gsp, gso, gsu, gsd, gdp, gdo, gdu, gdd = outs
-    gdp = gdp.reshape(rows, 4, 3, 256)[:, :, :, :192]
-    gdp = jnp.transpose(gdp, (0, 2, 1, 3)).reshape(rows, 2304)
     return (
         (out.reshape(tokens.shape), gin.reshape(tokens.shape), gsp, gso, gsu, gsd)
         + tuple(gsmall[:, i] for i in range(4))

time: 320 us -> 244 us (0.76)
  Pallas kernels: 293 us -> 226 us
  local copies, waits for them, and re-layouts: 22 us -> 12.7 us
    pallas_call x1, Pallas kernels: 293 us -> 226 us  [mega(): pl.pallas_call(kernel, out_shape=[jax.ShapeDtypeStruct(shape, dt) for _,...]
    another operation x8 -> x0, local copies, waits for them, and re-layouts: 5.97 us -> none  [local_fast(): jnp.stack([weights[i] for i in (4, 5, 6, 7, 12, 13, 14, 15)], axis=1)]
    reshape x5 -> x0, local copies, waits for them, and re-layouts: 3.36 us -> none  [the longest x1 1.17 us: local_fast(): gdp = gdp.reshape(rows, 4, 3, 256)[:, :, :, :192]]
    unnamed x29 -> x28, local copies, waits for them, and re-layouts: 6.87 us -> 8.74 us
where the time goes in v2:
time: 244 us; the launch traced here: 243 us
  Pallas kernels  226 us (93%)
  local copies, waits for them, and re-layouts  12.7 us (5%)
  other arithmetic  3.44 us (1%)
    pallas_call x1, Pallas kernels, mega(): pl.pallas_call(kernel, out_shape=[jax.ShapeDtypeStruct(shape, dt) for _,...  226 us
    unnamed x28, local copies, waits for them, and re-layouts  8.74 us

profile of v2, /device:TPU:1, one launch (start us, length us, event | category | flops | bytes accessed | tf_op | source)
XLA Modules:
  0.0 243.2 jit_solution(6298663041553122207)
XLA Ops:
  0.7 1.3 compare_convert_fusion.refs_3_
  1.9 0.7 constant_dynamic-slice_fusion
  2.7 0.1 lt.26
  2.8 0.7 fusion.1.refs_2_
  3.5 1.5 select_convert_fusion.refs_4_
  5.0 226.3 %shard_map.339 = (bf16[512,768]{1,0:T(8,128)(2,1)}, f32[512,768]{1,0:T(8,128)}, f32[24,256]{1,0:T(8,128)}, f32[24,2304]{1,0:T(8,128)}, f32[24,768]{1,0:T(8,128)}...) custom-call(bf16[512,768]{1,0:T(8,128)(2,1)} %bitcast.6, ...), custom_call_target="tpu_custom_call" | custom-call | tf_op jit(solution)/shard_map/pallas_call | solution.py:1284
  231.2 0.0 copy-start
  231.2 1.8 slice_reduce_fusion
  233.1 1.3 slice.35
  234.4 2.1 copy.49
  236.4 0.0 copy-done
  236.5 0.0 copy-start.6
  236.5 0.0 copy-start.8
  236.5 0.0 copy-start.3
  236.5 1.1 copy.50
  237.6 0.0 copy-done.6
  237.6 0.0 copy-start.1
  237.6 0.7 copy.51
  238.3 0.0 copy-done.8
  238.3 0.6 copy.52
  239.0 0.0 copy-done.4
  239.0 0.7 copy.53
  239.7 0.0 copy-done.3
  239.7 0.7 copy.54
  240.4 0.0 copy-done.5
  240.4 0.7 copy.55
  241.1 0.0 copy-done.7
  241.1 0.6 copy.56
  241.7 0.0 copy-done.2
  241.7 0.7 copy.57
  242.4 0.0 copy-done.1
  242.4 0.7 copy.58
  (9 shorter events, 0.0 us)
Async XLA Ops:
  231.2 5.2 %copy-start = (f32[512,768]{1,0:T(8,128)S(1)}, f32[512,768]{1,0:T(8,128)}, u32[]{:S(2)}) copy-start(f32[512,768]{1,0:T(8,128)} %get-tuple-element.31) | copy-start | bytes 4718596
  236.5 1.2 copy-start.6
  236.5 1.9 copy-start.8
  236.5 2.5 %copy-start.4 = (f32[24,3072]{1,0:T(8,128)S(1)}, f32[24,3072]{1,0:T(8,128)}, u32[]{:S(2)}) copy-start(f32[24,3072]{1,0:T(8,128)} %get-tuple-element.80) | copy-start | bytes 884740
  236.5 3.2 %copy-start.3 = (f32[96,768]{1,0:T(8,128)S(1)}, f32[96,768]{1,0:T(8,128)}, u32[]{:S(2)}) copy-start(f32[96,768]{1,0:T(8,128)} %get-tuple-element.81) | copy-start | bytes 884740
  237.6 2.8 %copy-start.5 = (f32[24,2304]{1,0:T(8,128)S(1)}, f32[24,2304]{1,0:T(8,128)}, u32[]{:S(2)}) copy-start(f32[24,2304]{1,0:T(8,128)} %get-tuple-element.86) | copy-start | bytes 663556
  237.6 3.5 %copy-start.7 = (f32[24,768]{1,0:T(8,128)S(1)}, f32[24,768]{1,0:T(8,128)}, u32[]{:S(2)}) copy-start(f32[24,768]{1,0:T(8,128)} %get-tuple-element.87) | copy-start | bytes 221188
  237.6 4.1 %copy-start.2 = (f32[24,3072]{1,0:T(8,128)S(1)}, f32[24,3072]{1,0:T(8,128)}, u32[]{:S(2)}) copy-start(f32[24,3072]{1,0:T(8,128)} %get-tuple-element.88) | copy-start | bytes 884740
  237.6 4.8 %copy-start.1 = (f32[96,768]{1,0:T(8,128)S(1)}, f32[96,768]{1,0:T(8,128)}, u32[]{:S(2)}) copy-start(f32[96,768]{1,0:T(8,128)} %get-tuple-element.89) | copy-start | bytes 884740

commit v3 on v2

--- a/solution.py
+++ b/solution.py
@@ -76,17 +76,12 @@
         self.t, self.ss, self.rs, self.pending = t, ss, rs, []
 
     def send(self, at, src, dst, dev):
-        d = remote(src, dst, self.ss.at[at], self.rs.at[at], dev)
+        d = remote(src, dst, self.ss, self.rs.at[at], dev)
         d.start()
         self.pending.append(d)
 
     def arrived(self, at, ref):
-        remote(ref, ref, self.ss.at[at], self.rs.at[at], self.t.sib).wait_recv()
-
-    def send_when(self, cond, at, src, dst, dev):
-        d = remote(src, dst, self.ss.at[at], self.rs.at[at], dev)
-        pl.when(cond)(d.start)
-        self.pending.append((cond, d))
+        remote(ref, ref, self.ss, self.rs.at[at], self.t.sib).wait_recv()
 
     def drain(self):
         for d in self.pending:
@@ -104,7 +99,7 @@
     def z_relay(self, at, at2, view):
         t = self.t
         two = view(pl.ds(t.pass_from, 2))
-        d = remote(two, two, self.ss.at[at2], self.rs.at[at2], t.tip)
+        d = remote(two, two, self.ss, self.rs.at[at2], t.tip)
 
         @pl.when(t.middle)
         def _():
@@ -141,11 +136,11 @@
 
     def pair(self):
         n2 = self.got.shape[1]
-        self.send((0, 0), self.far.at[:, off(self.t.o, n2)], self.got, self.t.sib)
+        self.send(5 * len(self.windows), self.far.at[:, off(self.t.o, n2)], self.got, self.t.sib)
 
     def join(self):
         t = self.t
-        self.arrived((0, 0), self.got)
+        self.arrived(5 * len(self.windows), self.got)
         join_pair(t, self.shard, self.got, self.tmp, self.w.at[t.c, t.z, t.q])
 
     def pick(self, k, *lead):
@@ -159,36 +154,34 @@
         return lambda at: self.pick(k, at, self.t.q)
 
     def spread(self, k):
-        self.z_spread((k, 1), self.view(k))
+        self.z_spread(5 * k, self.view(k))
 
     def relay(self, k):
-        self.z_relay((k, 1), (k, 9), self.view(k))
+        self.z_relay(5 * k, 5 * k + 1, self.view(k))
 
     def first(self, k):
         t = self.t
-        self.z_last((k, 1), (k, 9), self.view(k))
+        self.z_last(5 * k, 5 * k + 1, self.view(k))
         line = self.line(k, t.q)
-        self.send((k, 2), line, line, t.n1)
-        self.send((k, 4), line, line, t.sib)
+        self.send(5 * k + 2, line, line, t.n1)
+        self.send(5 * k + 4, line, line, t.sib)
 
     def second(self, k):
         t = self.t
         line, other = self.line(k, t.q), self.line(k, t.q1)
-        self.arrived((k, 2), other)
-        self.send((k, 3), line, line, t.n2)
-        self.send((k, 7), other, other, t.n2)
-        self.send((k, 5), other, other, t.sib)
+        self.arrived(5 * k + 2, other)
+        self.send(5 * k + 3, line, line, t.n2)
+        self.send(5 * k + 3, other, other, t.n2)
+        self.send(5 * k + 4, other, other, t.sib)
 
     def third(self, k):
         t = self.t
-        for i in (3, 7):
-            self.arrived((k, i), self.line(k, t.q))
-        for i, q in ((6, t.q2), (8, t.q12)):
-            self.send((k, i), self.line(k, q), self.line(k, q), t.sib)
+        self.arrived(5 * k + 3, self.pick(k, slice(None), pl.ds(0, 2)))
+        for q in (t.q2, t.q12):
+            self.send(5 * k + 4, self.line(k, q), self.line(k, q), t.sib)
 
     def finish(self, k):
-        for i in (4, 5, 6, 8):
-            self.arrived((k, i), self.line(k, self.t.q))
+        self.arrived(5 * k + 4, self.pick(k, slice(None), slice(None)))
 
 
 class LineGather(Sender):
@@ -201,18 +194,18 @@
         return lambda at: self.w.at[self.t.c, at, :, pl.ds(*cols)]
 
     def spread(self, k):
-        self.z_spread((k, 0), self.view(k))
+        self.z_spread(3 * k, self.view(k))
 
     def relay(self, k):
-        self.z_relay((k, 0), (k, 1), self.view(k))
+        self.z_relay(3 * k, 3 * k + 1, self.view(k))
 
     def first(self, k):
-        self.z_last((k, 0), (k, 1), self.view(k))
+        self.z_last(3 * k, 3 * k + 1, self.view(k))
         line = self.view(k)(slice(None))
-        self.send((k, 2), line, line, self.t.sib)
+        self.send(3 * k + 2, line, line, self.t.sib)
 
     def finish(self, k):
-        self.arrived((k, 2), self.view(k)(slice(None)))
+        self.arrived(3 * k + 2, self.view(k)(slice(None)))
 
 
 class DocGather(Sender):
@@ -325,10 +318,10 @@
         return ref.at[lead + (pl.ds(*rows), pl.ds(*cols))]
 
     def pair(self, k):
-        self.send((k, 0), self.cut(self.w, k, self.t.o), self.cut(self.rc, k), self.t.sib)
+        self.send(5 * k, self.cut(self.w, k, self.t.o), self.cut(self.rc, k), self.t.sib)
 
     def pair_rows(self, z):
-        self.send((z, 0), self.w.at[self.t.o, z], self.rc.at[z], self.t.sib)
+        self.send(5 * z, self.w.at[self.t.o, z], self.rc.at[z], self.t.sib)
 
     def add(self, k, q, part):
         (r, rn), (a, an) = self.windows[k]
@@ -343,48 +336,48 @@
         t = self.t
         if self.by_rows:
             for z in range(4 if k == 0 else 0):
-                self.arrived((z, 0), self.rc.at[z])
+                self.arrived(5 * z, self.rc.at[z])
         else:
-            self.arrived((k, 0), self.cut(self.rc, k))
+            self.arrived(5 * k, self.cut(self.rc, k))
         for i, q in ((0, t.q2), (1, t.q12)):
             self.add(k, q, self.rc.at[:, q])
             self.send(
-                (k, 1 + i), self.cut(self.w, k, t.c, slice(None), q), self.cut(self.r1, k, i, slice(None)), t.n2
+                5 * k + 1 + i, self.cut(self.w, k, t.c, slice(None), q), self.cut(self.r1, k, i, slice(None)), t.n2
             )
         for q in (t.q, t.q1):
             self.add(k, q, self.rc.at[:, q])
 
     def second(self, k):
         t = self.t
-        self.arrived((k, 2), self.cut(self.r1, k, 1, slice(None)))
+        self.arrived(5 * k + 2, self.cut(self.r1, k, 1, slice(None)))
         self.add(k, t.q1, self.r1.at[1])
-        self.send((k, 3), self.cut(self.w, k, t.c, slice(None), t.q1), self.cut(self.r2, k, slice(None)), t.n1)
-        self.arrived((k, 1), self.cut(self.r1, k, 0, slice(None)))
+        self.send(5 * k + 3, self.cut(self.w, k, t.c, slice(None), t.q1), self.cut(self.r2, k, slice(None)), t.n1)
+        self.arrived(5 * k + 1, self.cut(self.r1, k, 0, slice(None)))
         self.add(k, t.q, self.r1.at[0])
 
     def third(self, k):
         t = self.t
-        self.arrived((k, 3), self.cut(self.r2, k, slice(None)))
+        self.arrived(5 * k + 3, self.cut(self.r2, k, slice(None)))
         self.add(k, t.q, self.r2)
         for i in range(3):
-            self.send((k, 4), self.cut(self.w, k, t.c, t.zz[i], t.q), self.cut(self.r3, k, 2 - i), t.zn[i])
+            self.send(5 * k + 4, self.cut(self.w, k, t.c, t.zz[i], t.q), self.cut(self.r3, k, 2 - i), t.zn[i])
 
     def fourth(self, k):
         t = self.t
         (r, rn), (a, an) = self.windows[k]
-        self.arrived((k, 4), self.cut(self.r3, k, slice(None)))
+        self.arrived(5 * k + 4, self.cut(self.r3, k, slice(None)))
         total = self.w[t.c, t.z, t.q, r : r + rn, a : a + an].astype(F32)
         for i in range(3):
             total = total + self.r3[i, r : r + rn, a : a + an].astype(F32)
         self.fin[r : r + rn, a : a + an] = total
         if k == len(self.windows) - 1:
             rd = self.fin.shape[0] // 2
-            self.send((0, 5), self.fin.at[off(t.o, rd, 8)], self.fin2, t.sib)
+            self.send(5 * len(self.windows), self.fin.at[off(t.o, rd, 8)], self.fin2, t.sib)
 
     def fifth(self):
         t = self.t
         rd, n2 = self.fin2.shape
-        self.arrived((0, 5), self.fin2)
+        self.arrived(5 * len(self.windows), self.fin2)
         self.out[:, off(t.c, n2)] = self.fin[off(t.c, rd, 8), :]
         self.out[:, off(t.o, n2)] = self.fin2[...]
 
@@ -441,6 +434,8 @@
     "dpu": [((2, 4, 4, 48, 768), BF)],
     "do": [((2, 256, 384), BF)],
     "dd": [((2, 4, 192, 384), BF)],
+    "tmask": [((4, 128), F32)],
+    "dmask": [((1, 32), F32)],
     "vec": [((16, 768), F32)],
     "table": [((16, 2, 768), F32)],
     "pr": [((512, 2304), BF)],
@@ -473,23 +468,26 @@
     "flip": [((768, 128), F32)],
 }
 SEMS = {
-    "gs": (5, 4, 10),
-    "gr": (5, 4, 10),
-    "ds": (25,),
+    "gr0": (6,),
+    "gr1": (16,),
+    "gr2": (6,),
+    "gr3": (21,),
+    "gr4": (21,),
     "dr": (25,),
     "ls": (4,),
-    "rs": (5, 4, 6),
-    "rr": (5, 4, 6),
-    "xs": (12,),
-    "xr": (12,),
-    "fs": (3, 10),
-    "fr": (3, 10),
-    "es": (3, 3),
-    "er": (3, 3),
+    "rr0": (6,),
+    "rr1": (16,),
+    "rr2": (6,),
+    "rr3": (21,),
+    "rr4": (21,),
+    "xr": (9,),
+    "fr": (15,),
+    "er": (9,),
+    "ss": (14,),
     "os": (11,),
-    "ins": (13,),
+    "ins": (12,),
 }
-INS = ("tok", "cot", "tmask", "dmask", "small", "sp", "so", "su", "sd", "dp", "dout", "du", "ddown")
+INS = ("tok", "cot", "counts", "small", "sp", "so", "su", "sd", "dp", "dout", "du", "ddown")
 OUTS = (
     ("out", (512, 768), BF),
     ("gin", (512, 768), F32),
@@ -547,7 +545,7 @@
 
 def run(b):
     t = b.t
-    b.x = Sender(t, b.xs, b.xr)
+    b.x = Sender(t, b.ss.at[0], b.xr)
     b.flying, b.coming = {}, {}
     for i, name in enumerate(INS):
         d = pltpu.make_async_copy(b.far[name], getattr(b, name), b.ins.at[i])
@@ -560,7 +558,7 @@
     shards = (b.small, b.sp, b.so, b.su, b.sd)
     far = [b.far[name] for name in ("small", "sp", "so", "su", "sd")]
     gs = [
-        Gather(t, far[i], shards[i], b.w[i], b.got[i], b.fin[i], WINDOWS[i], b.gs.at[i], b.gr.at[i])
+        Gather(t, far[i], shards[i], b.w[i], b.got[i], b.fin[i], WINDOWS[i], b.ss.at[1 + i], getattr(b, f"gr{i}"))
         for i in range(5)
     ]
     dg = DocGather(
@@ -573,15 +571,15 @@
         b.dpu,
         b.do,
         b.dd,
-        b.ds,
+        b.ss.at[6],
         b.dr,
         b.ls,
     )
     for g in gs:
         g.pair()
     dg.pair()
-    b.f = Gather(t, None, None, b.fq, None, None, FACTOR_WINDOWS, b.fs, b.fr)
-    b.e = LineGather(t, b.fz, LINE_WINDOWS, b.es, b.er)
+    b.f = Gather(t, None, None, b.fq, None, None, FACTOR_WINDOWS, b.ss.at[7], b.fr)
+    b.e = LineGather(t, b.fz, LINE_WINDOWS, b.ss.at[8], b.er)
 
     events = [(g, k) for g in gs for k in range(len(g.windows))]
     lines = events + [(dg, k) for k in range(7)]
@@ -628,7 +626,8 @@
     dg.join()
     tick(1)
     pl.semaphore_wait(b.met2, 4)
-    b.ready("cot", "tok", "tmask", "dmask")
+    b.ready("cot", "tok", "counts")
+    masks_in(b)
     send_cotangents(b)
     tick(5)
     vectors_in(b)
@@ -641,10 +640,11 @@
     segment_mix(b)
     for j in range(4):
         segment_up(b, j)
-        tick(12 + j)
-        if j:
-            dg.plane(j - 1)
-    dg.plane(3)
+        if j < 3:
+            tick(12 + j)
+    for k in range(4):
+        dg.plane(k)
+    tick(15)
     tick(16)
     for k in range(4, 7):
         dg.plane(k)
@@ -652,6 +652,7 @@
     send_summaries(b, summary_rows(b))
     steps = document(b)
     segment_down(b, 0)
+    segment_down(b, 1)
     dg.share()
     for g in gs:
         g.drain()
@@ -659,13 +660,12 @@
         dg.finish(i)
     dg.drain()
     next(steps)
-    segment_down(b, 1)
-    next(steps)
     second_back(b)
     next(steps)
     hidden_back(b)
     next(steps)
     first_back(b)
+    next(steps)
     next(steps)
     next(steps, None)
     finish_output(b)
@@ -686,8 +686,8 @@
             b.fin2[i],
             out,
             WINDOWS[i],
-            b.rs.at[i],
-            b.rr.at[i],
+            b.ss.at[9 + i],
+            getattr(b, f"rr{i}"),
         )
         for i, out in enumerate((b.gsmall, b.gsp, b.gso, b.gsu, b.gsd))
     ]
@@ -793,6 +793,21 @@
     table = jnp.transpose(small[1].reshape(768, 128))[0:32]
     for i in range(16):
         b.table[i] = table[2 * i : 2 * i + 2]
+
+
+def masks_in(b):
+    t = b.t
+    rows = [b.counts[m : m + 1, :].astype(F32) for m in range(2)]
+    lane = lax.broadcasted_iota(jnp.int32, (1, 64), 1)
+    slot = lax.broadcasted_iota(jnp.int32, (1, 128), 1)
+    for m in range(2):
+        for s in range(2):
+            own = jnp.sum(jnp.where(lane == 2 * t.dev + s, rows[m], 0.0), axis=1, keepdims=True)
+            keep = (slot.astype(F32) < own) | (slot == 0)
+            b.tmask[2 * m + s : 2 * m + s + 1, :] = jnp.where(keep, 1.0, 0.0)
+    row = jnp.where(t.half == 0, rows[0], rows[1])
+    row = jnp.where(lax.div(t.z, 2) == 0, row[:, 0:32], row[:, 32:64])
+    b.dmask[...] = jnp.where(row > 0.0, 1.0, 0.0)
 
 
 def vec(b, i):
@@ -1297,18 +1312,37 @@
     )(*arrays)
 
 
+def hand_on_kernel(*refs):
+    n = (len(refs) - 2) // 3
+    src, dst, mid = refs[:n], refs[n : 2 * n], refs[2 * n : 3 * n]
+    ins = [pltpu.make_async_copy(src[i], mid[i], refs[-2].at[i]) for i in range(n)]
+    outs = [pltpu.make_async_copy(mid[i], dst[i], refs[-1].at[i]) for i in range(n)]
+    for d in ins:
+        d.start()
+    for i in range(n):
+        ins[i].wait()
+        outs[i].start()
+    for d in outs:
+        d.wait()
+
+
+def hand_on(*arrays):
+    an = pl.BlockSpec(memory_space=pl.ANY)
+    n = len(arrays)
+    return pl.pallas_call(
+        hand_on_kernel,
+        out_shape=[jax.ShapeDtypeStruct(item.shape, item.dtype) for item in arrays],
+        in_specs=[an] * n,
+        out_specs=[an] * n,
+        scratch_shapes=[pltpu.VMEM(item.shape, item.dtype) for item in arrays]
+        + [pltpu.SemaphoreType.DMA((n,))] * 2,
+        compiler_params=pltpu.CompilerParams(vmem_limit_bytes=63 * 2**20),
+    )(*arrays)
+
+
 def local_fast(tokens, token_counts, *rest):
     weights, cotangent = rest[:17], rest[17]
-    batches, segments, length, width = tokens.shape
-    device = lax.axis_index("seg") * 2 + lax.axis_index("rep")
-    own = lax.dynamic_slice(token_counts, (0, device * segments), (batches, segments)).reshape(-1)
-    slots = jnp.arange(length)
-    tmask = ((slots[None] < own[:, None]) | (slots[None] == 0)).astype(F32)
-    z = lax.div(lax.axis_index("seg"), 4)
-    doc = lax.dynamic_slice(
-        token_counts, (lax.rem(z, 2), lax.div(z, 2) * DOC_SEGS), (1, DOC_SEGS)
-    )
-    dmask = (doc > 0).astype(F32)
+    width = tokens.shape[-1]
     rows = weights[0].shape[0]
     lane = jnp.arange(256)[None]
     small = jnp.pad(weights[16], ((0, 0), (128, 96)))
@@ -1318,13 +1352,13 @@
     outs = mega(
         tokens.reshape(-1, width),
         cotangent.reshape(-1, width),
-        tmask,
-        dmask,
+        token_counts,
         small,
         *weights[:4],
         *weights[8:12],
     )
-    out, gin, gsmall, gsp, gso, gsu, gsd, gdp, gdo, gdu, gdd = outs
+    gsmall = outs[2]
+    out, gin, gsp, gso, gsu, gsd, gdp, gdo, gdu, gdd = hand_on(*outs[:2], *outs[3:])
     return (
         (out.reshape(tokens.shape), gin.reshape(tokens.shape), gsp, gso, gsu, gsd)
         + tuple(gsmall[:, i] for i in range(4))

time: 244 us -> 229 us (0.939)
  local copies, waits for them, and re-layouts: 12.7 us -> 1.43 us
    unnamed x28 -> x2, local copies, waits for them, and re-layouts: 8.74 us -> 0.01 us
    pallas_call x1, Pallas kernels: 226 us -> 222 us  [mega(): pl.pallas_call(kernel, out_shape=[jax.ShapeDtypeStruct(shape, dt) for _,...]
    pallas_call x0 -> x1, Pallas kernels: none -> 3.56 us  [hand_on(): pl.pallas_call(hand_on_kernel, out_shape=[jax.ShapeDtypeStruct(item.shape...]
where the time goes in v3:
time: 229 us
  Pallas kernels  225 us (98%)
    pallas_call x1, Pallas kernels, mega(): pl.pallas_call(kernel, out_shape=[jax.ShapeDtypeStruct(shape, dt) for _,...  222 us

profile of v3, /device:TPU:1, one launch (start us, length us, event | category | flops | bytes accessed | tf_op | source)
XLA Modules:
  0.0 228.9 jit_solution(6938586032107780181)
XLA Ops:
  0.7 1.5 select_convert_fusion.refs_3_
  2.2 221.7 %shard_map.339 = (bf16[512,768]{1,0:T(8,128)(2,1)}, f32[512,768]{1,0:T(8,128)}, f32[24,256]{1,0:T(8,128)}, f32[24,2304]{1,0:T(8,128)}, f32[24,768]{1,0:T(8,128)}...) custom-call(bf16[512,768]{1,0:T(8,128)(2,1)} %bitcast.4, ...), custom_call_target="tpu_custom_call" | custom-call | tf_op jit(solution)/shard_map/pallas_call | solution.py:1299
  223.9 0.0 copy-start
  223.9 3.6 %shard_map.340 = (bf16[512,768]{1,0:T(8,128)(2,1)}, f32[512,768]{1,0:T(8,128)}, f32[24,2304]{1,0:T(8,128)}, f32[24,768]{1,0:T(8,128)}, f32[24,3072]{1,0:T(8,128)...) custom-call(bf16[512,768]{1,0:T(8,128)(2,1)} %get-tuple-element.40.r, ...), custom_call_target="tpu_custom_call" | custom-call | tf_op jit(solution)/shard_map/pallas_call | solution.py:1332
  227.4 0.0 copy-done
  227.5 0.8 slice_reduce_fusion
  228.3 0.6 slice.35
  (4 shorter events, 0.0 us)
Async XLA Ops:
  223.9 3.6 %copy-start = (f32[24,256]{1,0:T(8,128)S(1)}, f32[24,256]{1,0:T(8,128)}, u32[]{:S(2)}) copy-start(f32[24,256]{1,0:T(8,128)} %get-tuple-element.56) | copy-start | bytes 73732

commit v4 on v3

--- a/solution.py
+++ b/solution.py
@@ -214,8 +214,7 @@
         self.far, self.shards, self.stages, self.gots, self.tmps = far, shards, stages, gots, tmps
         self.dpu, self.do, self.dd, self.ls = dpu, do, dd, ls
         main, down = stages
-        q = t.qq
-        self.views = [(lambda at, k=k: main.at[at, :, off(q[k], 768)]) for k in (1, 2, 3, 0)]
+        self.views = [(lambda at, k=k: dpu.at[t.c, at, k]) for k in range(4)]
         self.views.append(lambda at: main.at[at, :, pl.ds(3072, 384)])
         self.views += [(lambda at, j=j: down.at[at, pl.ds(96 * j, 96)]) for j in range(2)]
 
@@ -256,8 +255,21 @@
 
         join_pair(t, dd, self.gots[3], self.tmps[1], down.at[t.z])
 
+    def ranks(self):
+        t = self.t
+        main = self.stages[0]
+        for k in (1, 2, 3):
+            self.send(18, main.at[t.z, :, off(t.qq[k], 768)], self.dpu.at[t.c, t.z, t.q], t.plane[k])
+        d = pltpu.make_async_copy(main.at[t.z, :, off(t.q, 768)], self.dpu.at[t.c, t.z, t.q], self.ls.at[0])
+        d.start()
+        self.local = [d]
+
     def spread(self, k):
-        self.z_spread((4 + k), self.views[k])
+        t = self.t
+        if k == 0:
+            self.arrived(18, self.dpu.at[t.c, t.z, pl.ds(0, 3)])
+            self.local.pop().wait()
+        self.z_spread(4 + k, self.views[k])
 
     def relay(self, k):
         self.z_relay(4 + k, 11 + k, self.views[k])
@@ -266,15 +278,11 @@
         t = self.t
         main, down = self.stages
         self.z_last(4 + w, 11 + w, self.views[w])
-        if w == 0:
-            self.local = []
+        if w < 4:
+            return
         for k in (1, 2, 3, 0):
-            if w < 4 and k != (1, 2, 3, 0)[w]:
-                continue
             q = t.qq[k]
-            if w < 4:
-                src, dst, at = main.at[:, :, off(q, 768)], self.dpu.at[t.c, :, t.q], 18
-            elif w == 4:
+            if w == 4:
                 src, at = main.at[q, :, pl.ds(3072, 384)], 19
                 dst = self.do.at[t.c, pl.ds(pl.multiple_of(48 * t.q, 16), 48)]
             else:
@@ -289,7 +297,6 @@
 
     def share(self):
         t = self.t
-        self.arrived(18, self.dpu.at[t.c, :, pl.ds(0, 3)])
         self.arrived(19, self.do.at[t.c, pl.ds(0, 144)])
         for j in range(2):
             self.arrived(20 + j, self.dd.at[t.c, pl.ds(0, 3), pl.ds(0, 96)])
@@ -624,6 +631,7 @@
     tick(0)
     b.ready("dp", "dout", "du", "ddown")
     dg.join()
+    dg.ranks()
     tick(1)
     pl.semaphore_wait(b.met2, 4)
     b.ready("cot", "tok", "counts")
@@ -642,17 +650,12 @@
         segment_up(b, j)
         if j < 3:
             tick(12 + j)
-    for k in range(4):
-        dg.plane(k)
-    tick(15)
-    tick(16)
-    for k in range(4, 7):
+    for k in range(7):
         dg.plane(k)
     tick(17)
     send_summaries(b, summary_rows(b))
     steps = document(b)
-    segment_down(b, 0)
-    segment_down(b, 1)
+    segment_down(b)
     dg.share()
     for g in gs:
         g.drain()
@@ -835,19 +838,23 @@
     keep = b.tmask[seg : seg + 1, :] > 0.0
     rows = pl.ds(128 * seg, 128)
 
-    @pl.loop(0, 6)
-    def _(p):
-        q2 = b.pr[rows, off(p, 128)]
-        k2 = b.pr[rows, off(p + 6, 128)]
-        v2 = b.pr[rows, off(p + 12, 128)]
-        qs = jnp.concatenate((q2 * low, q2 * high), axis=0)
-        scores = jnp.where(keep, dot_rt(qs, k2) * 0.125, floor_score)
-        raised = jnp.exp(scores - jnp.max(scores, axis=-1, keepdims=True))
-        shares = (raised * (1.0 / jnp.sum(raised, axis=-1, keepdims=True))).astype(BF)
-        b.sh[6 * seg + p] = shares
-        both = dot(shares, v2)
-        lane = lax.broadcasted_iota(jnp.int32, (128, 128), 1)
-        b.ctx[rows, off(p, 128)] = jnp.where(lane < 64, both[:128], both[128:]).astype(BF)
+    lane = lax.broadcasted_iota(jnp.int32, (128, 128), 1)
+
+    @pl.loop(0, 3)
+    def _(i):
+        pairs = (2 * i, 2 * i + 1)
+        loaded = [[b.pr[rows, off(p + 6 * g, 128)] for g in range(3)] for p in pairs]
+        stacked = [jnp.concatenate((q2 * low, q2 * high), axis=0) for q2, _, _ in loaded]
+        scores = [
+            jnp.where(keep, dot_rt(qs, k2) * 0.125, floor_score)
+            for qs, (_, k2, _) in zip(stacked, loaded)
+        ]
+        raised = [jnp.exp(v - jnp.max(v, axis=-1, keepdims=True)) for v in scores]
+        shares = [(v * (1.0 / jnp.sum(v, axis=-1, keepdims=True))).astype(BF) for v in raised]
+        both = [dot(v, v2) for v, (_, _, v2) in zip(shares, loaded)]
+        for p, share, two in zip(pairs, shares, both):
+            b.sh[6 * seg + p] = share
+            b.ctx[rows, off(p, 128)] = jnp.where(lane < 64, two[:128], two[128:]).astype(BF)
 
 
 def segment_mix(b):
@@ -899,17 +906,24 @@
     return rows
 
 
-def segment_down(b, r):
-    w = b.w[4]
-    rows = pl.ds(256 * r, 256)
-
-    @pl.loop(0, 2)
-    def _(h):
-        b.row[rows, off(h, 384)] += dot(b.act[rows, :], w[h].reshape(3072, 384))
+def thirds(w, depth):
+    middle = jnp.concatenate((w[0, :, :, :, 256:384], w[1, :, :, :, 0:128]), axis=-1)
+    for part in (w[0, :, :, :, 0:256], middle, w[1, :, :, :, 128:384]):
+        yield part.reshape(depth, 256)
+
+
+def side_by_side(a, c, rows):
+    return jnp.concatenate((a.reshape(rows, 384), c.reshape(rows, 384)), axis=1)
+
+
+def segment_down(b):
+    for i, part in enumerate(thirds(b.w[4], 3072)):
+        cols = slice(256 * i, 256 * i + 256)
+        b.row[:, cols] += dot(b.act[...], part)
 
     gain, shift = vec(b, 2), vec(b, 3)
 
-    @pl.loop(8 * r, 8 * r + 8)
+    @pl.loop(0, 16, unroll=2)
     def _(i):
         rows = off(i, 32, 32)
         n, inverse = normed(b.row[rows, :])
@@ -1082,7 +1096,7 @@
         return gains + g * n, shifts + g
 
     zero = jnp.zeros((16, 768), F32)
-    gains, shifts = lax.fori_loop(0, 32, body, (zero, zero))
+    gains, shifts = lax.fori_loop(0, 32, body, (zero, zero), unroll=2)
     b.vg[2:3, :] = jnp.sum(gains, axis=0, keepdims=True)
     b.vg[3:4, :] = jnp.sum(shifts, axis=0, keepdims=True)
 
@@ -1112,9 +1126,7 @@
     @pl.loop(0, 4)
     def _(z):
         cols = off(z, 768)
-        back = dot_rt(b.lowc[:, 0:384], w[0, z].reshape(768, 384)) + dot_rt(
-            b.lowc[:, 384:768], w[1, z].reshape(768, 384)
-        )
+        back = dot_rt(b.lowc[...], side_by_side(w[0, z], w[1, z], 768))
         delta = (back * b.gpc[:, cols].astype(F32)).astype(BF)
         b.gpc[:, cols] = delta
         for s in range(4):
@@ -1140,9 +1152,7 @@
         cols = off(z, 768)
         for r in range(2):
             rows = pl.ds(256 * r, 256)
-            back = dot_rt(b.low[rows, 0:384], w[0, z].reshape(768, 384)) + dot_rt(
-                b.low[rows, 384:768], w[1, z].reshape(768, 384)
-            )
+            back = dot_rt(b.low[rows, :], side_by_side(w[0, z], w[1, z], 768))
             b.gp[rows, cols] = (back * b.gp[rows, cols].astype(F32)).astype(BF)
 
 
@@ -1180,7 +1190,7 @@
         return scales + g * n, offsets + g
 
     zero = jnp.zeros((16, 768), F32)
-    scales, offsets = lax.fori_loop(0, 32, body, (zero, zero))
+    scales, offsets = lax.fori_loop(0, 32, body, (zero, zero), unroll=2)
     b.vg[0:1, :] = jnp.sum(scales, axis=0, keepdims=True)
     b.vg[1:2, :] = jnp.sum(offsets, axis=0, keepdims=True)
 
@@ -1190,9 +1200,7 @@
     b.flying.pop("out").wait()
     for r in range(2):
         rows = pl.ds(256 * r, 256)
-        back = dot_rt(b.low[rows, 0:384], w[0].reshape(768, 384)) + dot_rt(
-            b.low[rows, 384:768], w[1].reshape(768, 384)
-        )
+        back = dot_rt(b.low[rows, :], side_by_side(w[0], w[1], 768))
         b.ob[rows, :] = back.astype(BF)
 
 
@@ -1200,24 +1208,27 @@
     low, high = lane_masks()
     rows = pl.ds(128 * seg, 128)
 
-    @pl.loop(0, 6)
-    def _(p):
-        q2 = b.pr[rows, off(p, 128)]
-        k2 = b.pr[rows, off(p + 6, 128)]
-        v2 = b.pr[rows, off(p + 12, 128)]
-        d2 = b.ob[rows, off(p, 128)]
-        qs = jnp.concatenate((q2 * low, q2 * high), axis=0)
-        cs = jnp.concatenate((d2 * low, d2 * high), axis=0)
-        shares_low = b.sh[6 * seg + p]
-        shares = shares_low.astype(F32)
-        shares_delta = dot_rt(cs, v2)
-        inner = jnp.sum(shares_delta * shares, axis=-1, keepdims=True)
-        scores_delta = (shares * (shares_delta - inner)).astype(BF)
-        dq = dot(scores_delta, k2) * 0.125
-        lane = lax.broadcasted_iota(jnp.int32, (128, 128), 1)
-        b.pr[rows, off(p, 128)] = jnp.where(lane < 64, dq[:128], dq[128:]).astype(BF)
-        b.pr[rows, off(p + 6, 128)] = (dot_lt(scores_delta, qs) * 0.125).astype(BF)
-        b.pr[rows, off(p + 12, 128)] = dot_lt(shares_low, cs).astype(BF)
+    lane = lax.broadcasted_iota(jnp.int32, (128, 128), 1)
+
+    @pl.loop(0, 3)
+    def _(i):
+        pairs = (2 * i, 2 * i + 1)
+        loaded = [[b.pr[rows, off(p + 6 * g, 128)] for g in range(3)] for p in pairs]
+        deltas = [b.ob[rows, off(p, 128)] for p in pairs]
+        shares = [b.sh[6 * seg + p] for p in pairs]
+        stacked = [jnp.concatenate((q2 * low, q2 * high), axis=0) for q2, _, _ in loaded]
+        cs = [jnp.concatenate((d2 * low, d2 * high), axis=0) for d2 in deltas]
+        back = [dot_rt(c, v2) for c, (_, _, v2) in zip(cs, loaded)]
+        wide = [v.astype(F32) for v in shares]
+        inner = [jnp.sum(d * v, axis=-1, keepdims=True) for d, v in zip(back, wide)]
+        ds = [(v * (d - n)).astype(BF) for v, d, n in zip(wide, back, inner)]
+        dq = [dot(d, k2) * 0.125 for d, (_, k2, _) in zip(ds, loaded)]
+        dk = [dot_lt(d, qs) * 0.125 for d, qs in zip(ds, stacked)]
+        dv = [dot_lt(v, c) for v, c in zip(shares, cs)]
+        for j, p in enumerate(pairs):
+            b.pr[rows, off(p, 128)] = jnp.where(lane < 64, dq[j][:128], dq[j][128:]).astype(BF)
+            b.pr[rows, off(p + 6, 128)] = dk[j].astype(BF)
+            b.pr[rows, off(p + 12, 128)] = dv[j].astype(BF)
 
 
 def input_back(b):

time: 229 us -> 220 us (0.961)
  Pallas kernels: 225 us -> 216 us
    pallas_call x1, Pallas kernels: 222 us -> 213 us  [mega(): pl.pallas_call(kernel, out_shape=[jax.ShapeDtypeStruct(shape, dt) for _,...]
where the time goes in v4:
time: 220 us
  Pallas kernels  216 us (98%)
    pallas_call x1, Pallas kernels, mega(): pl.pallas_call(kernel, out_shape=[jax.ShapeDtypeStruct(shape, dt) for _,...  213 us

profile of v4, /device:TPU:1, one launch (start us, length us, event | category | flops | bytes accessed | tf_op | source)
XLA Modules:
  0.0 219.7 jit_solution(11971496231113128781)
XLA Ops:
  0.7 1.5 select_convert_fusion.refs_3_
  2.2 212.5 %shard_map.339 = (bf16[512,768]{1,0:T(8,128)(2,1)}, f32[512,768]{1,0:T(8,128)}, f32[24,256]{1,0:T(8,128)}, f32[24,2304]{1,0:T(8,128)}, f32[24,768]{1,0:T(8,128)}...) custom-call(bf16[512,768]{1,0:T(8,128)(2,1)} %bitcast.4, ...), custom_call_target="tpu_custom_call" | custom-call | tf_op jit(solution)/shard_map/pallas_call | solution.py:1310
  214.7 0.0 copy-start
  214.7 3.6 %shard_map.340 = (bf16[512,768]{1,0:T(8,128)(2,1)}, f32[512,768]{1,0:T(8,128)}, f32[24,2304]{1,0:T(8,128)}, f32[24,768]{1,0:T(8,128)}, f32[24,3072]{1,0:T(8,128)...) custom-call(bf16[512,768]{1,0:T(8,128)(2,1)} %get-tuple-element.40.r, ...), custom_call_target="tpu_custom_call" | custom-call | tf_op jit(solution)/shard_map/pallas_call | solution.py:1343
  218.3 0.0 copy-done
  218.3 0.8 slice_reduce_fusion
  219.1 0.6 slice.35
  (4 shorter events, 0.0 us)
Async XLA Ops:
  214.7 3.6 %copy-start = (f32[24,256]{1,0:T(8,128)S(1)}, f32[24,256]{1,0:T(8,128)}, u32[]{:S(2)}) copy-start(f32[24,256]{1,0:T(8,128)} %get-tuple-element.56) | copy-start | bytes 73732
